TPU v7x, 128 devices: a whole 4x4x4 slice. The times are simulated.
128 devices in a mesh: gx: 32 (over x, z, core), gy: 4 (over y).
Axes of the slice: x: 4, y: 4, z: 4, core: 2. Of those that a mesh axis runs over, the one named last changes fastest.
Arguments:
- fine_features: bfloat16 [4096, 32, 512], P(('gx', 'gy')), may hold values from -6 to 6
- coarse_cache: bfloat16 [65536, 2048], P(('gx', 'gy')), may hold values from -6 to 6
- parent_owner: int32 [4096, 1], P(('gx', 'gy')), may hold values from 0 to 127; in each aligned block of 32 rows (0 to 31, 32 to 63, ...) at most 2 rows name the same one
- parent_cell: int32 [4096], P(('gx', 'gy')), may hold values from 0 to 511
- face_list: int32 [2560], P(('gx', 'gy')), may hold values from 0 to 31, as said below
- adjacency: int32 [4096, 26], P(('gx', 'gy')), may hold values from -1 to 51, as said below
- parent_proj: bfloat16 [32, 32], replicated, may hold values from -1 to 1
- conv_first: bfloat16 [27, 32, 32], replicated, may hold values from -0.21875 to 0.21875
- bias_first: float32 [32], replicated, may hold values from -3 to 3
- conv_second: bfloat16 [27, 32, 32], replicated, may hold values from -0.21875 to 0.21875
- bias_second: float32 [32], replicated, may hold values from -3 to 3
Outputs:
- level_out: bfloat16 [4096, 32, 512], P(('gx', 'gy'))
Inputs may be any that keep to these rules, and one draw needn't show every extreme that they name: `parent_owner`: among the bricks of one device no owner is named more than 2 times; some owner is named exactly 2 times. `face_list`: each device's 20 entries are four runs of local brick indices, distinct within a run: 8 bricks on its face toward higher x, 8 toward lower x, 2 toward higher y, 2 toward lower y. `adjacency`: entries 32 to 39 appear only in columns with dx = -1, the next 8 only with dx = 1, the next 2 only with dx = 0 and dy = -1, the last 2 only with dx = 0 and dy = 1.
All inputs are finite; a program needn't handle non-finite values.
Results may differ from a plain program's by a relative error of at most 0.0051.
Values may be sent and summed in bfloat16 or wider, within the bound.
A program may use at most 128 MiB of HBM per device.

v0:
```python
import jax
import jax.numpy as jnp
import numpy as np
from jax import lax
from jax.sharding import PartitionSpec as P


def with_halo(cells, sides, width):
    for axis, dim in sides:
        count = lax.axis_size(axis)
        ends = count - 1
        head = lax.slice_in_dim(cells, 0, width, axis=dim)
        tail = lax.slice_in_dim(cells, cells.shape[dim] - width, cells.shape[dim], axis=dim)
        cells = jnp.concatenate(
            [
                lax.ppermute(tail, axis, [(i, (i + 1) % count) for i in range(ends)]),
                cells,
                lax.ppermute(head, axis, [((i + 1) % count, i) for i in range(ends)]),
            ],
            axis=dim,
        )
    return cells


def halo_tiles(field, faces):
    bricks = field.shape[0]
    x_count = bricks // 4
    y_count = bricks // 16
    toward_high_x = faces[:x_count]
    toward_low_x = faces[x_count : 2 * x_count]
    toward_high_y = faces[2 * x_count : 2 * x_count + y_count]
    toward_low_y = faces[2 * x_count + y_count :]
    x_sent = jnp.concatenate([field[toward_low_x], field[toward_high_x]], axis=0)
    x_recv = with_halo(x_sent, (("gx", 0),), x_count)
    y_sent = jnp.concatenate([field[toward_low_y], field[toward_high_y]], axis=0)
    y_recv = with_halo(y_sent, (("gy", 0),), y_count)
    return jnp.concatenate(
        [x_recv[:x_count], x_recv[-x_count:], y_recv[:y_count], y_recv[-y_count:]], axis=0
    )


def cell_range(step):
    if step < 0:
        return (7, 8)
    if step == 0:
        return (0, 8)
    return (0, 1)


def build_tiles(field, extended, adjacency):
    bricks = field.shape[0]
    channels = field.shape[1]
    blank_row = extended.shape[0]
    whole = jnp.concatenate([extended, jnp.zeros((1, channels, 512), field.dtype)], axis=0)
    whole = whole.reshape(blank_row + 1, channels, 8, 8, 8)
    own_five = field.reshape(bricks, channels, 8, 8, 8)
    safe = jnp.where(adjacency >= 0, adjacency, blank_row)
    planes = []
    column = 0
    for i in range(3):
        rows_y = []
        for j in range(3):
            pieces = []
            for k in range(3):
                if i == 1 and j == 1 and (k == 1):
                    pieces.append(own_five)
                    continue
                xa, xb = cell_range(i - 1)
                ya, yb = cell_range(j - 1)
                za, zb = cell_range(k - 1)
                pieces.append(jnp.take(whole[:, :, xa:xb, ya:yb, za:zb], safe[:, column], axis=0))
                column += 1
            rows_y.append(jnp.concatenate(pieces, axis=4))
        planes.append(jnp.concatenate(rows_y, axis=3))
    return jnp.concatenate(planes, axis=2)


def layer(field, faces, adjacency, weights, bias):
    bricks = field.shape[0]
    channels = field.shape[1]
    outputs = weights.shape[1]
    halos = halo_tiles(field, faces)
    extended = jnp.concatenate([field, halos], axis=0)
    padded = build_tiles(field, extended, adjacency)
    kernel = weights.reshape(3, 3, 3, outputs, channels).transpose(3, 4, 0, 1, 2)
    result = lax.conv_general_dilated(
        padded,
        kernel,
        (1, 1, 1),
        "VALID",
        dimension_numbers=("NCDHW", "OIDHW", "NCDHW"),
        preferred_element_type=jnp.float32,
    )
    return result.reshape(bricks, outputs, 512) + bias[None, :, None]


def lookup(cache, cells):
    rows = jnp.take(cache, jnp.maximum(cells, 0), axis=0)
    return jnp.where((cells >= 0)[:, None], rows, jnp.zeros_like(rows))


def upsample_table():
    grid = np.arange(512)
    cell_of = 16 * (grid // 128) + 4 * (grid // 16 % 4) + grid % 8 // 2
    table = (np.arange(64)[:, None] == cell_of[None, :]).astype(np.float32)
    return table


def per_device(
    fine_features,
    coarse_cache,
    parent_owner,
    parent_cell,
    face_list,
    adjacency,
    parent_proj,
    conv_first,
    bias_first,
    conv_second,
    bias_second,
):
    bricks = fine_features.shape[0]
    channels = fine_features.shape[1]
    x_devices = lax.axis_size("gx")
    y_devices = lax.axis_size("gy")
    devices = x_devices * y_devices
    slot_count = max(2, 2 * bricks // devices)
    owners = parent_owner[:, 0]
    onehot = (owners[:, None] == jnp.arange(devices, dtype=jnp.int32)[None, :]).astype(jnp.int32)
    before = jnp.cumsum(onehot, axis=0) - onehot
    position = jnp.sum(before * onehot, axis=1)
    target = owners * slot_count + position
    requests = jnp.full((devices * slot_count,), -1, jnp.int32).at[target].set(parent_cell)
    arrived = lax.all_to_all(requests, ("gx", "gy"), split_axis=0, concat_axis=0, tiled=True)
    answers = lookup(coarse_cache, arrived)
    returned = lax.all_to_all(answers, ("gx", "gy"), split_axis=0, concat_axis=0, tiled=True)
    parent_rows = returned[target].reshape(bricks * channels, 64)
    spread_table = jnp.asarray(upsample_table()).astype(jnp.bfloat16)
    upsampled = jnp.dot(parent_rows, spread_table, preferred_element_type=jnp.float32).astype(
        jnp.bfloat16
    )
    upsampled = upsampled.reshape(bricks, channels, 512)
    mapped = jnp.einsum("oc,ncv->nov", parent_proj, upsampled, preferred_element_type=jnp.float32)
    level_in = (fine_features.astype(jnp.float32) + mapped).astype(jnp.bfloat16)
    hidden = jax.nn.silu(layer(level_in, face_list, adjacency, conv_first, bias_first)).astype(
        jnp.bfloat16
    )
    second = layer(hidden, face_list, adjacency, conv_second, bias_second)
    return (level_in.astype(jnp.float32) + second).astype(jnp.bfloat16)


def solution(mesh):
    placed = (
        P(("gx", "gy"), None, None),
        P(("gx", "gy"), None),
        P(("gx", "gy"), None),
        P(("gx", "gy")),
        P(("gx", "gy")),
        P(("gx", "gy"), None),
        P(),
        P(),
        P(),
        P(),
        P(),
    )
    return jax.shard_map(
        per_device,
        mesh=mesh,
        in_specs=placed,
        out_specs=P(("gx", "gy"), None, None),
        check_vma=False,
    )
```

profile of v0, /device:TPU:10, one launch (start us, length us, event | category | flops | bytes accessed | tf_op | source)
XLA Modules:
  0.0 513.8 jit_solution(5183640630180672709)
XLA Ops:
  4.0 10.4 %all-to-all-start = ((s32[128,2,1]{1,2,0:T(1,128)}), s32[128,2,1]{1,2,0:T(1,128)S(1)}, u32[]{:S(2)}, u32[]{:S(2)}) async-start(s32[128,2,1]{1,2,0:T(1,128)} %bitcast.3), calls=%async_computation | async-start | bytes 131072 | tf_op jit(solution)/shard_map/all_to_all | solution.py:134
  33.0 2.4 broadcast_select_fusion.1
  35.4 9.8 %all-to-all-start.1 = ((bf16[128,2,2048]{2,1,0:T(2,128)(2,1)}), bf16[128,2,2048]{2,1,0:T(2,128)(2,1)S(1)}, u32[]{:S(2)}, u32[]{:S(2)}) async-start(bf16[128,2,2048]{2,1,0:T(2,128)(2,1)} %broadcast_select_fusion.1), calls=%async_computation.1 | async-start | bytes 2097152 | tf_op jit(solution)/shard_map/all_to_all | solution.py:136
  48.0 14.8 %all-to-all-done.1 = bf16[128,2,2048]{2,1,0:T(2,128)(2,1)S(1)} async-done(((bf16[128,2,2048]{2,1,0:T(2,128)(2,1)}), bf16[128,2,2048]{2,1,0:T(2,128)(2,1)S(1)}, u32[]{:S(2)}, u32[]{:S(2)}) %all-to-all-start.1) | async-done | bytes 1048608 | tf_op jit(solution)/shard_map/all_to_all | solution.py:136
  66.8 2.2 collective-permute-start
  69.6 5.5 %collective-permute-start.1 = (bf16[8,32,512]{2,1,0:T(8,128)(2,1)S(1)}, bf16[8,32,512]{2,1,0:T(8,128)(2,1)}, u32[]{:S(2)}, u32[]{:S(2)}) collective-permute-start(bf16[8,32,512]{2,1,0:T(8,128)(2,1)S(1)} %gather_fusion.3), channel_id=1, source_target_pairs={{4,0},{8,4},{12,8},{16,12},{20,16},{24,20},{28,24},{32,28},{36,32}... | collective-permute-start | bytes 786440 | tf_op jit(solution)/shard_map/ppermute | solution.py:18
  75.8 6.4 %copy.568 = bf16[32,32,512]{1,0,2:T(8,128)(2,1)} copy(bf16[32,32,512]{2,1,0:T(8,128)(2,1)S(1)} %get-tuple-element.99) | data formatting | bytes 2097152 | tf_op jit(solution)/shard_map/reshape | solution.py:56
  83.3 2.1 collective-permute-start.2
  85.4 3.9 collective-permute-start.3
  91.7 3.8 copy.456
  96.7 3.0 fusion.122
  99.6 2.8 fusion.124
  102.4 2.3 fusion.123
  104.7 2.3 slice_bitcast_fusion.1
  107.0 3.1 fusion.125
  110.1 7.2 %copy.559 = bf16[53,32,512]{1,0,2:T(8,128)(2,1)} copy(bf16[53,32,512]{2,1,0:T(8,128)(2,1)S(1)} %constant_dynamic-update-slice_fusion) | data formatting | bytes 3473408 | tf_op jit(solution)/shard_map/reshape | solution.py:55
  118.0 1.7 copy.561
  119.7 1.7 copy.575
  121.4 1.7 copy.574
  123.2 1.7 copy.562
  124.9 1.7 copy.565
  126.6 1.7 copy.571
  128.3 1.7 copy.570
  130.0 1.7 copy.566
  131.7 3.4 copy.588
  135.2 3.4 copy.589
  138.6 4.0 copy.567
  142.6 3.4 copy.473
  146.1 2.4 copy.485
  180.0 1.9 gather_fusion.14
  182.9 1.9 gather_fusion.31
  186.0 1.9 gather_fusion.22
  189.2 1.9 gather_fusion.20
  192.2 1.9 gather_fusion.25
  202.3 25.5 %fusion.1.clone.4 = bf16[32,32,10,10,10]{1,0,4,3,2:T(8,128)(2,1)S(1)} fusion(bf16[32,32,1,1,1]{1,0,4,3,2:T(8,128)(2,1)S(1)} %bitcast_select_fusion.44, bf16[32,32,1,1,8]{1,0,4,3,2:T(8,128)(2,1)S(1)} %bitcast_select_fusion.24, bf16[32,32,1,1,1]{1,0,4,3,2:T(8,128)(2,1)S(1)} %bitcast_select_fusion.45, ...), kind=kLoop, calls=%fused_computation.65.clone.clone.clone.1 | loop fusion | flops 26624000 | bytes 4096000 | tf_op jit(solution)/shard_map/convert_element_type | solution.py:145
  227.8 94.0 %multiply_convert_fusion = (bf16[32,32,8,8,8]{0,1,4,3,2:T(8,128)(2,1)}, f32[32,32,8,8,8]{0,1,4,3,2:T(8,128)}) fusion(f32[32]{0:T(128)S(1)} %copy-done.54, bf16[3,3,3,32,32]{4,3,2,1,0:T(8,128)(2,1)S(1)} %bitcast.286, bf16[32,32,10,10,10]{1,0,4,3,2:T(8,128)(2,1)S(1)} %fusion.1.clone.4), kind=kOutput, calls=%fused_computation.63 | convolution fusion | flops 909115392 | bytes 5249152 | tf_op jit(solution)/shard_map/conv_general_dilated | solution.py:86
  321.8 6.6 %copy.503 = f32[32,32,512]{2,1,0:T(8,128)} copy(f32[32,32,512]{0,1,2:T(8,128)} %bitcast.259) | data formatting | bytes 4194304 | tf_op jit(solution)/shard_map/reshape | solution.py:94
  328.4 3.3 constant_dynamic-update-slice_fusion.11
  331.7 1.9 gather_fusion.6
  333.6 1.9 collective-permute-start.4
  335.6 1.9 gather_fusion.7
  337.5 5.8 %collective-permute-start.5 = (bf16[8,32,512]{2,1,0:T(8,128)(2,1)S(1)}, bf16[8,32,512]{2,1,0:T(8,128)(2,1)}, u32[]{:S(2)}, u32[]{:S(2)}) collective-permute-start(bf16[8,32,512]{2,1,0:T(8,128)(2,1)S(1)} %gather_fusion.7), channel_id=1, source_target_pairs={{4,0},{8,4},{12,8},{16,12},{20,16},{24,20},{28,24},{32,28},{36,32}... | collective-permute-start | bytes 786440 | tf_op jit(solution)/shard_map/ppermute | solution.py:18
  343.2 1.9 gather_fusion.9
  345.1 1.9 gather_fusion.8
  347.1 3.9 collective-permute-start.6
  351.0 1.9 collective-permute-start.7
  354.9 2.2 collective-permute-done.7
  357.2 3.8 copy.504
  361.0 1.8 fusion.116
  362.7 2.7 fusion.119
  365.5 2.1 fusion.117
  367.6 2.3 fusion.118
  369.9 2.3 fusion.120
  372.2 3.2 fusion.121
  375.4 7.2 %copy.578 = bf16[53,32,512]{1,0,2:T(8,128)(2,1)} copy(bf16[53,32,512]{2,1,0:T(8,128)(2,1)S(1)} %constant_dynamic-update-slice_fusion.6) | data formatting | bytes 3473408 | tf_op jit(solution)/shard_map/reshape | solution.py:55
  413.1 2.6 copy.605
  418.0 3.2 copy.598
  423.5 2.6 copy.596
  428.5 2.7 copy.601
  433.4 3.0 copy.599
  444.9 25.3 %fusion.136 = bf16[32,32,10,10,10]{0,1,4,3,2:T(8,128)(2,1)S(1)} fusion(bf16[32,32,1,1,1]{0,1,4,3,2:T(8,128)(2,1)S(1)} %bitcast_select_fusion.36, bf16[32,32,1,1,8]{0,1,4,3,2:T(8,128)(2,1)S(1)} %copy-done.9, bf16[32,32,1,1,1]{0,1,4,3,2:T(8,128)(2,1)S(1)} %bitcast_select_fusion.37, bf16[32,32,1,8,1]{0,1,4,3,2:T(8,128)(2,1)} %bitcast_select_fusion.13, ...), kind=kLoop, calls=%fused_computation.119.clone.1 | loop fusion | flops 26624000 | bytes 4096000 | tf_op jit(solution)/shard_map/conv_general_dilated | solution.py:86
  470.3 33.7 %fusion.54 = f32[32,32,8,8,8]{1,0,4,3,2:T(8,128)} fusion(bf16[3,3,3,32,32]{4,3,2,1,0:T(8,128)(2,1)S(1)} %bitcast.287, bf16[32,32,10,10,10]{0,1,4,3,2:T(8,128)(2,1)S(1)} %fusion.136), kind=kOutput, calls=%fused_computation.118 | convolution fusion | flops 905969664 | bytes 4200448 | tf_op jit(solution)/shard_map/conv_general_dilated | solution.py:86
  504.0 6.3 %copy.558 = f32[32,32,512]{2,1,0:T(8,128)} copy(f32[32,32,512]{1,0,2:T(8,128)} %bitcast.260) | data formatting | bytes 4194304 | tf_op jit(solution)/shard_map/reshape | solution.py:94
  510.3 3.0 add_convert_fusion
  (368 shorter events, 129.5 us)
Async XLA Ops:
  0.0 30.8 %copy-start = (bf16[512,2048]{1,0:T(8,128)(2,1)S(1)}, bf16[512,2048]{1,0:T(8,128)(2,1)}, u32[]{:S(2)}) copy-start(bf16[512,2048]{1,0:T(8,128)(2,1)} %param.27) | copy-start | bytes 6291460
  4.0 26.2 %all-to-all-start = ((s32[128,2,1]{1,2,0:T(1,128)}), s32[128,2,1]{1,2,0:T(1,128)S(1)}, u32[]{:S(2)}, u32[]{:S(2)}) async-start(s32[128,2,1]{1,2,0:T(1,128)} %bitcast.3), calls=%async_computation | async-start | bytes 131072 | tf_op jit(solution)/shard_map/all_to_all | solution.py:134
  30.2 38.9 %copy-start.15 = (s32[1024]{0:T(1024)}, s32[1024]{0:T(1024)S(1)}, u32[]{:S(2)}) copy-start(s32[1024]{0:T(1024)S(1)} %pad_clamp_fusion.28) | copy-start | bytes 12292
  30.9 33.3 %copy-start.13 = (bf16[64,512]{1,0:T(8,128)(2,1)S(1)}, bf16[64,512]{1,0:T(8,128)(2,1)}, u32[]{:S(2)}) copy-start(bf16[64,512]{1,0:T(8,128)(2,1)} %constant.94) | copy-start | bytes 196612
  30.9 33.7 %copy-start.14 = (bf16[32,32]{1,0:T(8,128)(2,1)S(1)}, bf16[32,32]{1,0:T(8,128)(2,1)}, u32[]{:S(2)}) copy-start(bf16[32,32]{1,0:T(8,128)(2,1)} %param.32) | copy-start | bytes 6148
  35.4 27.5 %all-to-all-start.1 = ((bf16[128,2,2048]{2,1,0:T(2,128)(2,1)}), bf16[128,2,2048]{2,1,0:T(2,128)(2,1)S(1)}, u32[]{:S(2)}, u32[]{:S(2)}) async-start(bf16[128,2,2048]{2,1,0:T(2,128)(2,1)} %broadcast_select_fusion.1), calls=%async_computation.1 | async-start | bytes 2097152 | tf_op jit(solution)/shard_map/all_to_all | solution.py:136
  45.2 37.0 %copy-start.16 = (s32[1024]{0:T(1024)}, s32[1024]{0:T(1024)S(1)}, u32[]{:S(2)}) copy-start(s32[1024]{0:T(1024)S(1)} %pad_clamp_fusion.29) | copy-start | bytes 12292
  66.8 22.5 %collective-permute-start = (bf16[8,32,512]{2,1,0:T(8,128)(2,1)S(1)}, bf16[8,32,512]{2,1,0:T(8,128)(2,1)}, u32[]{:S(2)}, u32[]{:S(2)}) collective-permute-start(bf16[8,32,512]{2,1,0:T(8,128)(2,1)S(1)} %gather_fusion.2), channel_id=1, source_target_pairs={{0,4},{4,8},{8,12},{12,16},{16,20},{20,24},{24,28},{28,32},{32,36}... | collective-permute-start | bytes 786440 | tf_op jit(solution)/shard_map/ppermute | solution.py:16
  69.1 26.5 %copy-start.17 = (s32[1024]{0:T(1024)}, s32[1024]{0:T(1024)S(1)}, u32[]{:S(2)}) copy-start(s32[1024]{0:T(1024)S(1)} %pad_clamp_fusion.26) | copy-start | bytes 12292
  69.6 20.7 %collective-permute-start.1 = (bf16[8,32,512]{2,1,0:T(8,128)(2,1)S(1)}, bf16[8,32,512]{2,1,0:T(8,128)(2,1)}, u32[]{:S(2)}, u32[]{:S(2)}) collective-permute-start(bf16[8,32,512]{2,1,0:T(8,128)(2,1)S(1)} %gather_fusion.3), channel_id=1, source_target_pairs={{4,0},{8,4},{12,8},{16,12},{20,16},{24,20},{28,24},{32,28},{36,32}... | collective-permute-start | bytes 786440 | tf_op jit(solution)/shard_map/ppermute | solution.py:18
  75.2 20.4 %copy-start.18 = (s32[1024]{0:T(1024)}, s32[1024]{0:T(1024)S(1)}, u32[]{:S(2)}) copy-start(s32[1024]{0:T(1024)S(1)} %pad_clamp_fusion.27) | copy-start | bytes 12292
  83.3 8.0 %collective-permute-start.2 = (bf16[2,32,512]{2,1,0:T(8,128)(2,1)S(1)}, bf16[2,32,512]{2,1,0:T(8,128)(2,1)S(1)}, u32[]{:S(2)}, u32[]{:S(2)}) collective-permute-start(bf16[2,32,512]{2,1,0:T(8,128)(2,1)S(1)} %gather_fusion.4), channel_id=1, source_target_pairs={{0,1},{1,2},{2,3},{4,5},{5,6},{6,7},{8,9},{9,10},{10,11},{12,13},{... | collective-permute-start | bytes 196616 | tf_op jit(solution)/shard_map/ppermute | solution.py:16
  85.4 6.3 %collective-permute-start.3 = (bf16[2,32,512]{2,1,0:T(8,128)(2,1)S(1)}, bf16[2,32,512]{2,1,0:T(8,128)(2,1)S(1)}, u32[]{:S(2)}, u32[]{:S(2)}) collective-permute-start(bf16[2,32,512]{2,1,0:T(8,128)(2,1)S(1)} %gather_fusion.5), channel_id=1, source_target_pairs={{1,0},{2,1},{3,2},{5,4},{6,5},{7,6},{9,8},{10,9},{11,10},{13,12},{... | collective-permute-start | bytes 196616 | tf_op jit(solution)/shard_map/ppermute | solution.py:18
  95.5 11.4 %copy-start.3 = (bf16[53,32,512]{0,2,1:T(8,128)(2,1)S(1)}, bf16[53,32,512]{0,2,1:T(8,128)(2,1)}, u32[]{:S(2)}) copy-start(bf16[53,32,512]{0,2,1:T(8,128)(2,1)} %copy.456) | copy-start | bytes 5210116
  117.3 28.7 %copy-start.6 = (bf16[53,32,8,8]{0,3,2,1:T(8,128)(2,1)S(1)}, bf16[53,32,8,8]{0,3,2,1:T(8,128)(2,1)}, u32[]{:S(2)}) copy-start(bf16[53,32,8,8]{0,3,2,1:T(8,128)(2,1)} %get-tuple-element.89) | copy-start | bytes 651268
  117.3 31.2 %copy-start.4 = (bf16[53,32,8,8,1]{0,4,3,2,1:T(2,128)(2,1)S(1)}, bf16[53,32,8,8,1]{0,4,3,2,1:T(2,128)(2,1)}, u32[]{:S(2)}) copy-start(bf16[53,32,8,8,1]{0,4,3,2,1:T(2,128)(2,1)} %get-tuple-element.91) | copy-start | bytes 651268
  153.0 31.9 %copy-start.20 = (pred[32]{0:T(512)(128)(4,1)S(1)}, pred[32]{0:T(512)(128)(4,1)}, u32[]{:S(2)}) copy-start(pred[32]{0:T(512)(128)(4,1)} %get-tuple-element.133) | copy-start | bytes 100
  172.7 15.2 %copy-start.35 = (pred[32]{0:T(512)(128)(4,1)S(1)}, pred[32]{0:T(512)(128)(4,1)}, u32[]{:S(2)}) copy-start(pred[32]{0:T(512)(128)(4,1)} %get-tuple-element.142) | copy-start | bytes 100
  184.8 9.3 %copy-start.29 = (pred[32]{0:T(512)(128)(4,1)S(1)}, pred[32]{0:T(512)(128)(4,1)}, u32[]{:S(2)}) copy-start(pred[32]{0:T(512)(128)(4,1)} %get-tuple-element.139) | copy-start | bytes 100
  188.0 9.2 %copy-start.50 = (pred[32]{0:T(512)(128)(4,1)S(1)}, pred[32]{0:T(512)(128)(4,1)}, u32[]{:S(2)}) copy-start(pred[32]{0:T(512)(128)(4,1)} %get-tuple-element.128) | copy-start | bytes 100
  189.1 9.6 %copy-start.42 = (pred[32]{0:T(512)(128)(4,1)S(1)}, pred[32]{0:T(512)(128)(4,1)}, u32[]{:S(2)}) copy-start(pred[32]{0:T(512)(128)(4,1)} %get-tuple-element.131) | copy-start | bytes 100
  189.1 10.4 %copy-start.48 = (pred[32]{0:T(512)(128)(4,1)S(1)}, pred[32]{0:T(512)(128)(4,1)}, u32[]{:S(2)}) copy-start(pred[32]{0:T(512)(128)(4,1)} %get-tuple-element.135) | copy-start | bytes 100
  189.1 11.1 %copy-start.46 = (pred[32]{0:T(512)(128)(4,1)S(1)}, pred[32]{0:T(512)(128)(4,1)}, u32[]{:S(2)}) copy-start(pred[32]{0:T(512)(128)(4,1)} %get-tuple-element.137) | copy-start | bytes 100
  189.1 11.8 %copy-start.52 = (pred[32]{0:T(512)(128)(4,1)S(1)}, pred[32]{0:T(512)(128)(4,1)}, u32[]{:S(2)}) copy-start(pred[32]{0:T(512)(128)(4,1)} %compare_and_fusion.18) | copy-start | bytes 100
  189.1 12.4 %copy-start.38 = (pred[32]{0:T(512)(128)(4,1)S(1)}, pred[32]{0:T(512)(128)(4,1)}, u32[]{:S(2)}) copy-start(pred[32]{0:T(512)(128)(4,1)} %get-tuple-element.147) | copy-start | bytes 100
  189.1 13.1 %copy-start.40 = (pred[32]{0:T(512)(128)(4,1)S(1)}, pred[32]{0:T(512)(128)(4,1)}, u32[]{:S(2)}) copy-start(pred[32]{0:T(512)(128)(4,1)} %get-tuple-element.151) | copy-start | bytes 100
  202.3 25.5 %copy-start.54 = (f32[32]{0:T(128)S(1)}, f32[32]{0:T(128)}, u32[]{:S(2)}) copy-start(f32[32]{0:T(128)} %param.34) | copy-start | bytes 388
  202.3 25.5 %copy-start.56 = (bf16[27,32,32]{2,1,0:T(8,128)(2,1)S(1)}, bf16[27,32,32]{2,1,0:T(8,128)(2,1)}, u32[]{:S(2)}) copy-start(bf16[27,32,32]{2,1,0:T(8,128)(2,1)} %param.33) | copy-start | bytes 165892
  333.6 19.3 %collective-permute-start.4 = (bf16[8,32,512]{2,1,0:T(8,128)(2,1)S(1)}, bf16[8,32,512]{2,1,0:T(8,128)(2,1)}, u32[]{:S(2)}, u32[]{:S(2)}) collective-permute-start(bf16[8,32,512]{2,1,0:T(8,128)(2,1)S(1)} %gather_fusion.6), channel_id=1, source_target_pairs={{0,4},{4,8},{8,12},{12,16},{16,20},{20,24},{24,28},{28,32},{32,36}... | collective-permute-start | bytes 786440 | tf_op jit(solution)/shard_map/ppermute | solution.py:16
  337.5 16.4 %collective-permute-start.5 = (bf16[8,32,512]{2,1,0:T(8,128)(2,1)S(1)}, bf16[8,32,512]{2,1,0:T(8,128)(2,1)}, u32[]{:S(2)}, u32[]{:S(2)}) collective-permute-start(bf16[8,32,512]{2,1,0:T(8,128)(2,1)S(1)} %gather_fusion.7), channel_id=1, source_target_pairs={{4,0},{8,4},{12,8},{16,12},{20,16},{24,20},{28,24},{32,28},{36,32}... | collective-permute-start | bytes 786440 | tf_op jit(solution)/shard_map/ppermute | solution.py:18
  347.1 7.8 %collective-permute-start.6 = (bf16[2,32,512]{2,1,0:T(8,128)(2,1)S(1)}, bf16[2,32,512]{2,1,0:T(8,128)(2,1)S(1)}, u32[]{:S(2)}, u32[]{:S(2)}) collective-permute-start(bf16[2,32,512]{2,1,0:T(8,128)(2,1)S(1)} %gather_fusion.8), channel_id=1, source_target_pairs={{0,1},{1,2},{2,3},{4,5},{5,6},{6,7},{8,9},{9,10},{10,11},{12,13},{... | collective-permute-start | bytes 196616 | tf_op jit(solution)/shard_map/ppermute | solution.py:16
  351.0 6.2 %collective-permute-start.7 = (bf16[2,32,512]{2,1,0:T(8,128)(2,1)S(1)}, bf16[2,32,512]{2,1,0:T(8,128)(2,1)S(1)}, u32[]{:S(2)}, u32[]{:S(2)}) collective-permute-start(bf16[2,32,512]{2,1,0:T(8,128)(2,1)S(1)} %gather_fusion.9), channel_id=1, source_target_pairs={{1,0},{2,1},{3,2},{5,4},{6,5},{7,6},{9,8},{10,9},{11,10},{13,12},{... | collective-permute-start | bytes 196616 | tf_op jit(solution)/shard_map/ppermute | solution.py:18
  361.0 11.2 %copy-start.2 = (bf16[53,32,512]{0,2,1:T(8,128)(2,1)S(1)}, bf16[53,32,512]{0,2,1:T(8,128)(2,1)}, u32[]{:S(2)}) copy-start(bf16[53,32,512]{0,2,1:T(8,128)(2,1)} %copy.504) | copy-start | bytes 5210116
  369.9 16.8 %copy-start.26 = (pred[32]{0:T(512)(128)(4,1)S(1)}, pred[32]{0:T(512)(128)(4,1)}, u32[]{:S(2)}) copy-start(pred[32]{0:T(512)(128)(4,1)} %get-tuple-element.146) | copy-start | bytes 100
  372.2 17.0 %copy-start.31 = (pred[32]{0:T(512)(128)(4,1)S(1)}, pred[32]{0:T(512)(128)(4,1)}, u32[]{:S(2)}) copy-start(pred[32]{0:T(512)(128)(4,1)} %get-tuple-element.130) | copy-start | bytes 100
  372.2 19.5 %copy-start.32 = (pred[32]{0:T(512)(128)(4,1)S(1)}, pred[32]{0:T(512)(128)(4,1)}, u32[]{:S(2)}) copy-start(pred[32]{0:T(512)(128)(4,1)} %get-tuple-element.136) | copy-start | bytes 100
  375.3 27.5 %copy-start.37 = (pred[32]{0:T(512)(128)(4,1)S(1)}, pred[32]{0:T(512)(128)(4,1)}, u32[]{:S(2)}) copy-start(pred[32]{0:T(512)(128)(4,1)} %get-tuple-element.138) | copy-start | bytes 100
  375.3 29.1 %copy-start.24 = (pred[32]{0:T(512)(128)(4,1)S(1)}, pred[32]{0:T(512)(128)(4,1)}, u32[]{:S(2)}) copy-start(pred[32]{0:T(512)(128)(4,1)} %get-tuple-element.150) | copy-start | bytes 100
  375.3 30.8 %copy-start.22 = (pred[32]{0:T(512)(128)(4,1)S(1)}, pred[32]{0:T(512)(128)(4,1)}, u32[]{:S(2)}) copy-start(pred[32]{0:T(512)(128)(4,1)} %get-tuple-element.148) | copy-start | bytes 100
  375.3 32.4 %copy-start.25 = (pred[32]{0:T(512)(128)(4,1)S(1)}, pred[32]{0:T(512)(128)(4,1)}, u32[]{:S(2)}) copy-start(pred[32]{0:T(512)(128)(4,1)} %get-tuple-element.134) | copy-start | bytes 100
  382.5 26.9 %copy-start.23 = (pred[32]{0:T(512)(128)(4,1)S(1)}, pred[32]{0:T(512)(128)(4,1)}, u32[]{:S(2)}) copy-start(pred[32]{0:T(512)(128)(4,1)} %get-tuple-element.132) | copy-start | bytes 100
  382.5 27.5 %copy-start.5 = (bf16[53,32,1,8,8]{0,4,3,2,1:T(8,128)(2,1)S(1)}, bf16[53,32,1,8,8]{0,4,3,2,1:T(8,128)(2,1)}, u32[]{:S(2)}) copy-start(bf16[53,32,1,8,8]{0,4,3,2,1:T(8,128)(2,1)} %get-tuple-element.64) | copy-start | bytes 651268
  388.3 24.7 %copy-start.19 = (pred[32]{0:T(512)(128)(4,1)S(1)}, pred[32]{0:T(512)(128)(4,1)}, u32[]{:S(2)}) copy-start(pred[32]{0:T(512)(128)(4,1)} %get-tuple-element.149) | copy-start | bytes 100
  406.8 10.4 %copy-start.21 = (pred[32]{0:T(512)(128)(4,1)S(1)}, pred[32]{0:T(512)(128)(4,1)}, u32[]{:S(2)}) copy-start(pred[32]{0:T(512)(128)(4,1)} %get-tuple-element.133) | copy-start | bytes 100
  413.1 9.6 %copy-start.36 = (pred[32]{0:T(512)(128)(4,1)S(1)}, pred[32]{0:T(512)(128)(4,1)}, u32[]{:S(2)}) copy-start(pred[32]{0:T(512)(128)(4,1)} %get-tuple-element.142) | copy-start | bytes 100
  417.1 10.4 %copy-start.34 = (pred[32]{0:T(512)(128)(4,1)S(1)}, pred[32]{0:T(512)(128)(4,1)}, u32[]{:S(2)}) copy-start(pred[32]{0:T(512)(128)(4,1)} %get-tuple-element.144) | copy-start | bytes 100
  422.0 10.6 %copy-start.30 = (pred[32]{0:T(512)(128)(4,1)S(1)}, pred[32]{0:T(512)(128)(4,1)}, u32[]{:S(2)}) copy-start(pred[32]{0:T(512)(128)(4,1)} %get-tuple-element.139) | copy-start | bytes 100
  427.5 10.3 %copy-start.28 = (pred[32]{0:T(512)(128)(4,1)S(1)}, pred[32]{0:T(512)(128)(4,1)}, u32[]{:S(2)}) copy-start(pred[32]{0:T(512)(128)(4,1)} %get-tuple-element.141) | copy-start | bytes 100
  428.4 11.2 %copy-start.51 = (pred[32]{0:T(512)(128)(4,1)S(1)}, pred[32]{0:T(512)(128)(4,1)}, u32[]{:S(2)}) copy-start(pred[32]{0:T(512)(128)(4,1)} %get-tuple-element.128) | copy-start | bytes 100
  428.4 12.0 %copy-start.45 = (pred[32]{0:T(512)(128)(4,1)S(1)}, pred[32]{0:T(512)(128)(4,1)}, u32[]{:S(2)}) copy-start(pred[32]{0:T(512)(128)(4,1)} %get-tuple-element.129) | copy-start | bytes 100
  428.4 12.8 %copy-start.43 = (pred[32]{0:T(512)(128)(4,1)S(1)}, pred[32]{0:T(512)(128)(4,1)}, u32[]{:S(2)}) copy-start(pred[32]{0:T(512)(128)(4,1)} %get-tuple-element.131) | copy-start | bytes 100
  428.4 13.7 %copy-start.49 = (pred[32]{0:T(512)(128)(4,1)S(1)}, pred[32]{0:T(512)(128)(4,1)}, u32[]{:S(2)}) copy-start(pred[32]{0:T(512)(128)(4,1)} %get-tuple-element.135) | copy-start | bytes 100
  428.4 14.3 %copy-start.47 = (pred[32]{0:T(512)(128)(4,1)S(1)}, pred[32]{0:T(512)(128)(4,1)}, u32[]{:S(2)}) copy-start(pred[32]{0:T(512)(128)(4,1)} %get-tuple-element.137) | copy-start | bytes 100
  428.4 15.0 %copy-start.53 = (pred[32]{0:T(512)(128)(4,1)S(1)}, pred[32]{0:T(512)(128)(4,1)}, u32[]{:S(2)}) copy-start(pred[32]{0:T(512)(128)(4,1)} %compare_and_fusion.18) | copy-start | bytes 100
  428.4 15.7 %copy-start.39 = (pred[32]{0:T(512)(128)(4,1)S(1)}, pred[32]{0:T(512)(128)(4,1)}, u32[]{:S(2)}) copy-start(pred[32]{0:T(512)(128)(4,1)} %get-tuple-element.147) | copy-start | bytes 100
  428.4 16.4 %copy-start.41 = (pred[32]{0:T(512)(128)(4,1)S(1)}, pred[32]{0:T(512)(128)(4,1)}, u32[]{:S(2)}) copy-start(pred[32]{0:T(512)(128)(4,1)} %get-tuple-element.151) | copy-start | bytes 100
  428.4 16.4 %copy-start.7 = (bf16[32,32,1,1,8]{0,1,4,3,2:T(8,128)(2,1)S(1)}, bf16[32,32,1,1,8]{0,1,4,3,2:T(8,128)(2,1)}, u32[]{:S(2)}) copy-start(bf16[32,32,1,1,8]{0,1,4,3,2:T(8,128)(2,1)} %bitcast_select_fusion.23) | copy-start | bytes 49156
  428.4 16.4 %copy-start.8 = (bf16[32,32,1,1,8]{0,1,4,3,2:T(8,128)(2,1)S(1)}, bf16[32,32,1,1,8]{0,1,4,3,2:T(8,128)(2,1)}, u32[]{:S(2)}) copy-start(bf16[32,32,1,1,8]{0,1,4,3,2:T(8,128)(2,1)} %bitcast_select_fusion.20) | copy-start | bytes 49156
  428.5 16.4 %copy-start.9 = (bf16[32,32,1,1,8]{0,1,4,3,2:T(8,128)(2,1)S(1)}, bf16[32,32,1,1,8]{0,1,4,3,2:T(8,128)(2,1)}, u32[]{:S(2)}) copy-start(bf16[32,32,1,1,8]{0,1,4,3,2:T(8,128)(2,1)} %bitcast_select_fusion.12) | copy-start | bytes 49156
  428.5 16.4 %copy-start.10 = (bf16[32,32,1,1,8]{0,1,4,3,2:T(8,128)(2,1)S(1)}, bf16[32,32,1,1,8]{0,1,4,3,2:T(8,128)(2,1)}, u32[]{:S(2)}) copy-start(bf16[32,32,1,1,8]{0,1,4,3,2:T(8,128)(2,1)} %bitcast_select_fusion.15) | copy-start | bytes 49156
  428.5 16.4 %copy-start.11 = (bf16[32,32,8,1,1]{0,1,4,3,2:T(8,128)(2,1)S(1)}, bf16[32,32,8,1,1]{0,1,4,3,2:T(8,128)(2,1)}, u32[]{:S(2)}) copy-start(bf16[32,32,8,1,1]{0,1,4,3,2:T(8,128)(2,1)} %bitcast_select_fusion.19) | copy-start | bytes 49156
  428.5 16.4 %copy-start.12 = (bf16[32,32,8,1,1]{0,1,4,3,2:T(8,128)(2,1)S(1)}, bf16[32,32,8,1,1]{0,1,4,3,2:T(8,128)(2,1)}, u32[]{:S(2)}) copy-start(bf16[32,32,8,1,1]{0,1,4,3,2:T(8,128)(2,1)} %bitcast_select_fusion.17) | copy-start | bytes 49156
  444.9 25.3 %copy-start.57 = (bf16[27,32,32]{2,1,0:T(8,128)(2,1)S(1)}, bf16[27,32,32]{2,1,0:T(8,128)(2,1)}, u32[]{:S(2)}) copy-start(bf16[27,32,32]{2,1,0:T(8,128)(2,1)} %param.35) | copy-start | bytes 165892
  470.3 43.1 %copy-start.1 = (bf16[512,2048]{1,0:T(8,128)(2,1)S(1)}, bf16[512,2048]{1,0:T(8,128)(2,1)}, u32[]{:S(2)}) copy-start(bf16[512,2048]{1,0:T(8,128)(2,1)} %param.27) | copy-start | bytes 6291460
  (4 other events, 32.5 us)
where the time goes:
time: 523 us; the launch traced here: 514 us
  local copies, waits for them, and re-layouts  204 us (39%)
  matrix products  130 us (25%)
  other arithmetic  114 us (22%)
  starting transfers between devices  47.4 us (9%)
  waiting for transfers between devices  17.4 us (3%)
    conv_general_dilated x2, matrix products, layer(): lax.conv_general_dilated(padded, kernel, (1, 1, 1), 'VALID', dimension_nu...  128 us
    gather x78, local copies, waits for them, and re-layouts, build_tiles(): jnp.take(whole[:, :, xa:xb, ya:yb, za:zb], safe[:, column], axis=0)  55.8 us
    unnamed x144, local copies, waits for them, and re-layouts  33.9 us
    select_n x78, other arithmetic, build_tiles(): jnp.take(whole[:, :, xa:xb, ya:yb, za:zb], safe[:, column], axis=0)  33.6 us
    another operation x20, local copies, waits for them, and re-layouts, build_tiles(): jnp.take(whole[:, :, xa:xb, ya:yb, za:zb], safe[:, column], axis=0)  30.8 us
    slice x10, local copies, waits for them, and re-layouts, build_tiles(): whole[:, :, xa:xb, ya:yb, za:zb]  25.6 us
    convert_element_type x1, other arithmetic, per_device(): jax.nn.silu(layer(level_in, face_list, adjacency, conv_first, bias_first))  25.5 us
    conv_general_dilated x1, other arithmetic, layer(): lax.conv_general_dilated(padded, kernel, (1, 1, 1), 'VALID', dimension_nu...  25.3 us
  transfers between devices with their start and end apart: 10, of which 3 were waited for; matrix products, arithmetic and copies ran while one was open for 7% of the time, Pallas kernels for 0%

commit v1 on v0

v1 whole, which is shorter than its diff:
```python
import functools

import jax
import jax.numpy as jnp
import numpy as np
from jax import lax
from jax.experimental import pallas as pl
from jax.experimental.pallas import tpu as pltpu
from jax.sharding import PartitionSpec as P

F32 = jnp.float32
BF16 = jnp.bfloat16
NB = 32
SLOTS = 45
BLANK = 44
MESH = pl.DeviceIdType.MESH


def column_of(dx, dy, dz):
    at = 9 * (dx + 1) + 3 * (dy + 1) + dz + 1
    return at if at < 13 else at - 1


def lane_tables():
    lane = np.arange(512)
    z = 4 * (lane // 64 % 2) + lane // 128
    x, y = lane % 64 // 8, lane % 8
    voxel = 64 * x + 8 * y + z
    cell = 16 * (x // 2) + 4 * (y // 2) + z // 2
    perm = (np.arange(512)[:, None] == voxel[None, :]).astype(np.float32)
    up = (np.arange(64)[:, None] == cell[None, :]).astype(np.float32)
    blank = np.zeros_like(up)
    even = np.concatenate([up, blank], 0)
    odd = np.concatenate([blank, up], 0)
    return perm, np.concatenate([even, odd], 1)


def strips_of(weights):
    w = weights.reshape(3, 3, 3, 32, 32)[:, :, ::-1]
    w = w.transpose(0, 1, 4, 2, 3).reshape(9, 32, 96)
    return jnp.pad(w, ((0, 0), (0, 0), (0, 160)))


def build_band(strip_ref, band_ref):
    lane = lax.broadcasted_iota(jnp.int32, (32, 256), 1)
    zero = jnp.zeros((32, 256), F32)

    def per_x(i, carry):
        first, last = [], []
        for j in range(3):
            strip = strip_ref[3 * i + j].astype(F32)
            for z in range(8):
                rolled = strip if z == 1 else pltpu.roll(strip, (32 * (z - 1)) % 256, 1)
                if z == 0:
                    first.append(jnp.where(lane >= 224, rolled, zero))
                    rolled = jnp.where(lane >= 224, zero, rolled)
                if z == 7:
                    last.append(jnp.where(lane < 32, rolled, zero))
                    rolled = jnp.where(lane < 32, zero, rolled)
                band_ref[i, pl.ds(256 * j + 32 * z, 32), :] = rolled.astype(BF16)
        order = [first[0], first[1], last[1], last[0], first[2], zero, zero, last[2]]
        for n, part in enumerate(order):
            band_ref[i, pl.ds(768 + 32 * n, 32), :] = part.astype(BF16)
        return carry

    lax.fori_loop(0, 3, per_x, 0)


def edge_lanes(low, high):
    lane = lax.broadcasted_iota(jnp.int32, low.shape, 1)
    a = jnp.where(lane < 32, low, pltpu.roll(low, 32, 1))
    b = jnp.where(lane < 96, pltpu.roll(high, 96, 1), high)
    return jnp.where(lane < 64, a, b)


def kernel(
    fine_ref, ret_ref, target_ref, adj_ref, face_ref, proj_ref, perm_ref, unperm_ref, up_ref,
    strip1_ref, bias1_ref, strip2_ref, bias2_ref, out_ref,
    tile_ref, edge_ref, pad_ref, band1_ref, band2_ref, level_ref, par_ref, even_ref, odd_ref,
    sum_ref, mix_ref, xs_ref, ys_ref, yrow_ref, xr_ref, yr_ref, send_sem, recv_sem,
):
    gx, gy = lax.axis_index("gx"), lax.axis_index("gy")
    nx, ny = lax.axis_size("gx"), lax.axis_size("gy")
    up_x, down_x = lax.rem(gx + 1, nx), lax.rem(gx + nx - 1, nx)
    up_y, down_y = lax.rem(gy + 1, ny), lax.rem(gy + ny - 1, ny)
    neighbours = [(up_x, gy), (down_x, gy), (gx, up_y), (gx, down_y)]
    barrier = pltpu.get_barrier_semaphore()
    for other in neighbours:
        pl.semaphore_signal(barrier, inc=1, device_id=other, device_id_type=MESH)
    pl.semaphore_wait(barrier, 4)

    build_band(strip1_ref, band1_ref)
    build_band(strip2_ref, band2_ref)
    for x in range(8):
        tile_ref[x, BLANK] = jnp.zeros((8, 256), F32)
        edge_ref[x, BLANK] = jnp.zeros((8, 128), F32)

    wide = jnp.concatenate([proj_ref[...]] * 8, axis=0)
    chan = lax.broadcasted_iota(jnp.int32, (32, 256), 0)
    lane = lax.broadcasted_iota(jnp.int32, (32, 256), 1)
    pick = jnp.where(chan == 2 * (lane % 16) + lane // 128, 1.0, 0.0).astype(BF16)
    spread = jnp.dot(wide, pick, preferred_element_type=F32)
    row = lax.broadcasted_iota(jnp.int32, (256, 256), 0)
    lane = lax.broadcasted_iota(jnp.int32, (256, 256), 1)
    mix_ref[...] = jnp.where(row // 32 == lane % 128 // 16, spread, 0.0).astype(BF16)

    def place(x, slot, tile):
        tile_ref[x, slot] = tile
        edge_ref[x, slot] = edge_lanes(tile[:, :128], tile[:, 128:])

    def fetch(b, carry):
        par_ref[pl.ds(pl.multiple_of(16 * b, 16), 16), :] = ret_ref[target_ref[b]]
        return carry

    lax.fori_loop(0, NB, fetch, 0)

    def level(g, carry):
        rows = pl.ds(pl.multiple_of(256 * g, 256), 256)
        pair = par_ref[pl.ds(pl.multiple_of(128 * g, 128), 128), :]
        both = jnp.dot(pair, up_ref[...], preferred_element_type=F32).astype(BF16)
        stack = jnp.concatenate([both[:, :512], both[:, 512:]], axis=0)
        mapped = jnp.dot(mix_ref[...], stack, preferred_element_type=F32)
        fine = jnp.dot(fine_ref[rows, :], perm_ref[...], preferred_element_type=F32)
        rounded = (fine + mapped).astype(BF16)
        level_ref[rows, :] = rounded
        wide = rounded.astype(F32)
        for n in range(8):
            own = wide[32 * n : 32 * n + 32, :]
            square = jnp.concatenate([own[:, 128 * k : 128 * k + 128] for k in range(4)], axis=0)
            turned = square.T
            for x in range(8):
                low, high = turned[8 * x : 8 * x + 8], turned[64 + 8 * x : 72 + 8 * x]
                place(x, 8 * g + n, jnp.concatenate([low, high], axis=1))
        return carry

    lax.fori_loop(0, 4, level, 0)

    row8 = lax.broadcasted_iota(jnp.int32, (8, 256), 0)
    row8e = lax.broadcasted_iota(jnp.int32, (8, 128), 0)
    lane8e = lax.broadcasted_iota(jnp.int32, (8, 128), 1)

    def exchange(turn):
        for d in range(2):
            x = 7 if d == 0 else 0
            for j in range(0, 8, 2):
                two = jnp.concatenate(
                    [tile_ref[x, face_ref[8 * d + j]], tile_ref[x, face_ref[8 * d + j + 1]]], axis=0
                )
                xs_ref[turn, d, pl.ds(8 * j, 16), :] = two.astype(BF16)
            y = 7 if d == 0 else 0
            for j in range(2):
                at = face_ref[16 + 2 * d + j]
                for x in range(8):
                    yrow_ref[pl.ds(8 * j + x, 1), :] = tile_ref[x, at, pl.ds(y, 1), :]
            ys_ref[turn, d] = yrow_ref[...].astype(BF16)
        copies = []
        for d in range(2):
            copies.append(pltpu.make_async_remote_copy(
                src_ref=xs_ref.at[turn, d], dst_ref=xr_ref.at[turn, d],
                send_sem=send_sem.at[turn, d], recv_sem=recv_sem.at[turn, d],
                device_id=neighbours[d], device_id_type=MESH))
            copies.append(pltpu.make_async_remote_copy(
                src_ref=ys_ref.at[turn, d], dst_ref=yr_ref.at[turn, d],
                send_sem=send_sem.at[turn, 2 + d], recv_sem=recv_sem.at[turn, 2 + d],
                device_id=neighbours[2 + d], device_id_type=MESH))
        for copy in copies:
            copy.start()
        return copies

    def land(turn, copies):
        for copy in copies:
            copy.wait()
        for d in range(2):
            here = (gx > 0) if d == 0 else (gx < nx - 1)
            for j in range(8):
                if j % 2 == 0:
                    two = xr_ref[turn, d, pl.ds(8 * j, 16), :].astype(F32)
                    two = jnp.where(here, two, 0.0)
                place(7 if d == 0 else 0, 32 + j, two[8 * (j % 2) : 8 * (j % 2) + 8])
            here = (gy > 0) if d == 0 else (gy < ny - 1)
            rows = jnp.where(here, yr_ref[turn, d].astype(F32), 0.0)
            for j in range(2):
                for x in range(8):
                    line = rows[8 * j + x : 8 * j + x + 1]
                    place(x, 40 + 2 * d + j, jnp.broadcast_to(line, (8, 256)))

    def padded_tile(b, px):
        dx = -1 if px == 0 else (1 if px == 9 else 0)
        x = 7 if px == 0 else (0 if px == 9 else px - 1)

        def at(dy, dz):
            if dx == 0 and dy == 0 and dz == 0:
                return b
            return adj_ref[b * 26 + column_of(dx, dy, dz)]

        mid = tile_ref[x, at(0, 0)]
        low = pltpu.roll(jnp.where(row8 == 7, tile_ref[x, at(-1, 0)], mid), 1, 0)
        high = pltpu.roll(jnp.where(row8 == 0, tile_ref[x, at(1, 0)], mid), 7, 0)
        ends = [
            jnp.where(lane8e < 64, edge_ref[x, at(dy, 1)], edge_ref[x, at(dy, -1)])
            for dy in (-1, 0, 1)
        ]
        elow = pltpu.roll(jnp.where(row8e == 7, ends[0], ends[1]), 1, 0)
        ehigh = pltpu.roll(jnp.where(row8e == 0, ends[2], ends[1]), 7, 0)
        emid = jnp.where((lane8e >= 32) & (lane8e < 96), ends[1], elow)
        return jnp.concatenate([low, mid, high, emid, ehigh], axis=1)

    def pad_all():
        def per_pair(n, carry):
            for px in range(10):
                two = jnp.concatenate([padded_tile(2 * n, px), padded_tile(2 * n + 1, px)], axis=0)
                pad_ref[px, pl.ds(pl.multiple_of(16 * n, 16), 16), :] = two.astype(BF16)
            return carry

        lax.fori_loop(0, NB // 2, per_pair, 0)

    def conv(x, band_ref, bias_ref):
        total = jnp.dot(pad_ref[x], band_ref[0], preferred_element_type=F32)
        total += jnp.dot(pad_ref[x + 1], band_ref[1], preferred_element_type=F32)
        total += jnp.dot(pad_ref[x + 2], band_ref[2], preferred_element_type=F32)
        return total + bias_ref[...]

    land(0, exchange(0))
    pad_all()

    def first(x, carry):
        v = conv(x, band1_ref, bias1_ref)
        h = (v / (1.0 + jnp.exp(-v))).astype(BF16).astype(F32)
        tile_ref[x, pl.ds(0, NB)] = h.reshape(NB, 8, 256)
        e = edge_lanes(h[:, :128], h[:, 128:])
        edge_ref[x, pl.ds(0, NB)] = e.reshape(NB, 8, 128)
        return carry

    lax.fori_loop(0, 8, first, 0)
    land(1, exchange(1))
    pad_all()

    def second(x, carry):
        sum_ref[x] = conv(x, band2_ref, bias2_ref).reshape(NB, 8, 256)
        return carry

    lax.fori_loop(0, 8, second, 0)

    def finish(g, carry):
        rows = pl.ds(pl.multiple_of(256 * g, 256), 256)
        parts = []
        for n in range(8):
            tall = [sum_ref[x, 8 * g + n] for x in range(8)]
            turned = jnp.concatenate([t[:, :128] for t in tall] + [t[:, 128:] for t in tall], axis=0).T
            parts.append(jnp.concatenate([turned[32 * k : 32 * k + 32] for k in range(4)], axis=1))
        total = jnp.concatenate(parts, axis=0) + level_ref[rows, :].astype(F32)
        out = jnp.dot(total.astype(BF16), unperm_ref[...], preferred_element_type=F32)
        out_ref[rows, :] = out.astype(BF16)
        return carry

    lax.fori_loop(0, 4, finish, 0)


def lookup(cache, cells):
    rows = jnp.take(cache, jnp.maximum(cells, 0), axis=0)
    return jnp.where((cells >= 0)[:, None], rows, jnp.zeros_like(rows))


def per_device(
    fine_features, coarse_cache, parent_owner, parent_cell, face_list, adjacency,
    parent_proj, conv_first, bias_first, conv_second, bias_second,
):
    devices = lax.axis_size("gx") * lax.axis_size("gy")
    owners = parent_owner[:, 0]
    onehot = (owners[:, None] == jnp.arange(devices, dtype=jnp.int32)[None, :]).astype(jnp.int32)
    before = jnp.cumsum(onehot, axis=0) - onehot
    position = jnp.sum(before * onehot, axis=1)
    target = owners * 2 + position
    requests = jnp.full((devices * 2,), -1, jnp.int32).at[target].set(parent_cell)
    arrived = lax.all_to_all(requests, ("gx", "gy"), split_axis=0, concat_axis=0, tiled=True)
    answers = lookup(coarse_cache, arrived)
    returned = lax.all_to_all(answers, ("gx", "gy"), split_axis=0, concat_axis=0, tiled=True)
    returned = returned.reshape(devices * 2, 16, 128)
    places = jnp.where(adjacency < 0, BLANK, jnp.where(adjacency >= 40, adjacency - 8, adjacency))
    perm, up = lane_tables()
    vmem = pl.BlockSpec(memory_space=pltpu.VMEM)
    smem = pl.BlockSpec(memory_space=pltpu.SMEM)
    out = pl.pallas_call(
        kernel,
        out_shape=jax.ShapeDtypeStruct((NB * 32, 512), BF16),
        in_specs=[vmem, vmem, smem, smem, smem] + [vmem] * 8,
        out_specs=vmem,
        scratch_shapes=[
            pltpu.VMEM((8, SLOTS, 8, 256), F32),
            pltpu.VMEM((8, SLOTS, 8, 128), F32),
            pltpu.VMEM((10, 256, 1024), BF16),
            pltpu.VMEM((3, 1024, 256), BF16),
            pltpu.VMEM((3, 1024, 256), BF16),
            pltpu.VMEM((NB * 32, 512), BF16),
            pltpu.VMEM((NB * 16, 128), BF16),
            pltpu.VMEM((8, 128), BF16),
            pltpu.VMEM((8, 128), BF16),
            pltpu.VMEM((8, NB, 8, 256), F32),
            pltpu.VMEM((256, 256), BF16),
            pltpu.VMEM((2, 2, 64, 256), BF16),
            pltpu.VMEM((2, 2, 16, 256), BF16),
            pltpu.VMEM((16, 256), F32),
            pltpu.VMEM((2, 2, 64, 256), BF16),
            pltpu.VMEM((2, 2, 16, 256), BF16),
            pltpu.SemaphoreType.DMA((2, 4)),
            pltpu.SemaphoreType.DMA((2, 4)),
        ],
        compiler_params=pltpu.CompilerParams(
            collective_id=0, has_side_effects=True, vmem_limit_bytes=56 * 1024 * 1024
        ),
    )(
        fine_features.reshape(NB * 32, 512), returned, target, places.reshape(-1), face_list, parent_proj,
        jnp.asarray(perm, BF16), jnp.asarray(perm.T, BF16), jnp.asarray(up, BF16),
        strips_of(conv_first), jnp.tile(bias_first, 8)[None, :],
        strips_of(conv_second), jnp.tile(bias_second, 8)[None, :],
    )
    return out.reshape(NB, 32, 512)


def solution(mesh):
    placed = (
        P(("gx", "gy"), None, None),
        P(("gx", "gy"), None),
        P(("gx", "gy"), None),
        P(("gx", "gy")),
        P(("gx", "gy")),
        P(("gx", "gy"), None),
        P(),
        P(),
        P(),
        P(),
        P(),
    )
    return jax.shard_map(
        per_device,
        mesh=mesh,
        in_specs=placed,
        out_specs=P(("gx", "gy"), None, None),
        check_vma=False,
    )
```

time: 523 us -> 93.4 us (0.18)
  the two profiles are of different devices: /device:TPU:10 before, /device:TPU:0 now
where the time goes in v1:
time: 93.4 us; the launch traced here: 92.9 us
  Pallas kernels  35.2 us (38%)
  local copies, waits for them, and re-layouts  20.4 us (22%)
  blocking collectives  20.1 us (22%)
  other arithmetic  6.32 us (7%)
  waiting for transfers between devices  5.98 us (6%)
  starting transfers between devices  4.65 us (5%)
    pallas_call x1, Pallas kernels, per_device(): pl.pallas_call(kernel, out_shape=jax.ShapeDtypeStruct((NB * 32, 512), BF1...  35.2 us
    all_to_all x1, blocking collectives, per_device(): lax.all_to_all(requests, ('gx', 'gy'), split_axis=0, concat_axis=0, tiled...  20.1 us
    all_to_all x1, waiting for transfers between devices, per_device(): lax.all_to_all(answers, ('gx', 'gy'), split_axis=0, concat_axis=0, tiled=...  5.98 us
    all_to_all x1, starting transfers between devices, per_device(): lax.all_to_all(answers, ('gx', 'gy'), split_axis=0, concat_axis=0, tiled=...  4.65 us
    rev x2, local copies, waits for them, and re-layouts, strips_of(): w = weights.reshape(3, 3, 3, 32, 32)[:, :, ::-1]  4.35 us
    select_n x1, other arithmetic, lookup(): return jnp.where((cells >= 0)[:, None], rows, jnp.zeros_like(rows))  3.27 us
    gather x2, local copies, waits for them, and re-layouts, lookup(): rows = jnp.take(cache, jnp.maximum(cells, 0), axis=0)  2.86 us
    reshape x2, local copies, waits for them, and re-layouts, strips_of(): w = weights.reshape(3, 3, 3, 32, 32)[:, :, ::-1]  2.71 us
  transfers between devices with their start and end apart: 1, of which 1 were waited for; matrix products, arithmetic and copies ran while one was open for 14% of the time, Pallas kernels for 0%

profile of v1, /device:TPU:0, one launch (start us, length us, event | category | flops | bytes accessed | tf_op | source)
XLA Modules:
  0.0 92.9 jit_solution(14011705872428128048)
XLA Ops:
  0.0 0.0 copy-start
  0.0 0.9 fusion.1
  0.9 0.1 reduce_window_sum.11
  0.9 0.8 select_reduce_fusion
  1.8 0.7 fusion.2
  2.4 0.8 scatter_custom_fusion
  3.2 0.1 all_to_all.10
  3.4 20.1 %all_to_all.15 = s32[128,2,1]{1,2,0:T(1,128)S(1)} all-to-all(s32[128,2,1]{1,2,0:T(1,128)S(1)} %bitcast.25), channel_id=1, replica_groups=mesh['gx'=32,'gy'=4] {'gx','gy'}, dimensions={0} | all-to-all | bytes 2048 | tf_op jit(solution)/shard_map/all_to_all | solution.py:275
  23.5 0.1 copy.30
  23.6 0.1 copy.31
  23.8 0.1 copy.33
  23.9 0.1 copy.34
  24.0 0.1 reshape.82
  24.2 0.0 copy-done
  24.2 1.4 %gather_fusion = bf16[256,2048]{1,0:T(8,128)(2,1)S(1)} fusion(bf16[512,2048]{1,0:T(8,128)(2,1)S(1)} %copy-done, s32[1024]{0:T(1024)S(1)} %pad_clamp_fusion), kind=kCustom, calls=%fused_computation | custom fusion | bytes 2098176 | tf_op jit(solution)/shard_map/jit(_take)/gather | solution.py:260
  25.6 1.5 %gather.7 = bf16[128,2,2048]{2,1,0:T(2,128)(2,1)} reshape(bf16[256,2048]{1,0:T(8,128)(2,1)S(1)} %gather_fusion) | data formatting | bytes 2097152 | tf_op jit(solution)/shard_map/jit(_take)/gather | solution.py:260
  27.1 0.0 copy-start.1
  27.1 3.3 %broadcast_select_fusion.1 = bf16[128,2,2048]{2,1,0:T(2,128)(2,1)} fusion(pred[128,2]{1,0:T(8,128)(4,1)S(1)} %copy.31, bf16[128,2,2048]{2,1,0:T(2,128)(2,1)} %gather.7, pred[128,2]{1,0:T(8,128)(4,1)S(1)} %copy.33), kind=kLoop, calls=%fused_computation.3 | loop fusion | flops 1048576 | bytes 2097664 | tf_op jit(solution)/shard_map/jit(_where)/select_n | solution.py:261
  30.3 4.7 %all-to-all-start.1 = ((bf16[128,2,2048]{2,1,0:T(2,128)(2,1)}), bf16[128,2,2048]{2,1,0:T(2,128)(2,1)S(1)}, u32[]{:S(2)}, u32[]{:S(2)}) async-start(bf16[128,2,2048]{2,1,0:T(2,128)(2,1)} %broadcast_select_fusion.1), calls=%async_computation.1 | async-start | bytes 2097152 | tf_op jit(solution)/shard_map/all_to_all | solution.py:277
  35.0 0.0 copy-start.2
  35.0 0.0 copy-start.4
  35.0 0.0 copy-start.5
  35.0 0.0 copy-start.3
  35.0 0.0 copy-done.1
  35.0 0.9 copy.35
  35.9 2.2 %rev.6 = bf16[3,3,3,32,32]{3,2,4,1,0:T(4,128)(2,1)S(1)} reverse(bf16[3,3,3,32,32]{3,2,4,1,0:T(4,128)(2,1)} %copy.35), dimensions={2} | reverse | bytes 110592 | tf_op jit(solution)/shard_map/rev | solution.py:39
  38.1 0.2 reshape.76
  38.3 1.8 %copy.36 = bf16[3,3,3,32,32]{3,2,4,1,0:T(4,128)(2,1)} copy(bf16[3,3,3,32,32]{4,3,2,1,0:T(8,128)(2,1)} %bitcast.27) | data formatting | bytes 110592 | tf_op jit(solution)/shard_map/reshape | solution.py:39
  40.1 2.2 %rev.7 = bf16[3,3,3,32,32]{3,2,4,1,0:T(4,128)(2,1)S(1)} reverse(bf16[3,3,3,32,32]{3,2,4,1,0:T(4,128)(2,1)} %copy.36), dimensions={2} | reverse | bytes 110592 | tf_op jit(solution)/shard_map/rev | solution.py:39
  42.3 0.8 reshape.78
  43.1 0.7 pad.7.strip1_ref
  43.8 1.6 %pad.8.strip2_ref = bf16[9,32,256]{2,1,0:T(8,128)(2,1)} pad(bf16[9,32,96]{2,1,0:T(8,128)(2,1)} %reshape.78, bf16[]{:T(256)} %constant.43.clone.1), padding=0_0x0_0x0_160 | pad | bytes 202754 | tf_op jit(solution)/shard_map/jit(_pad)/pad | solution.py:41
  45.3 0.0 copy-done.2
  45.3 0.7 reshape.74.adj_ref
  46.0 0.0 copy-done.4
  46.0 0.7 broadcast_in_dim_tile.6.bias1_ref
  46.7 0.0 copy-done.5
  46.7 0.7 broadcast_in_dim_tile.7.bias2_ref
  47.3 0.0 copy-done.3
  47.4 0.6 multiply_add_fusion.target_ref
  47.9 6.0 %all-to-all-done.1 = bf16[128,2,2048]{2,1,0:T(2,128)(2,1)S(1)} async-done(((bf16[128,2,2048]{2,1,0:T(2,128)(2,1)}), bf16[128,2,2048]{2,1,0:T(2,128)(2,1)S(1)}, u32[]{:S(2)}, u32[]{:S(2)}) %all-to-all-start.1) | async-done | bytes 1048608 | tf_op jit(solution)/shard_map/all_to_all | solution.py:277
  53.9 1.5 %reshape.73.ret_ref = bf16[256,16,128]{2,1,0:T(8,128)(2,1)} reshape(bf16[128,2,2048]{2,1,0:T(2,128)(2,1)S(1)} %all-to-all-done.1) | data formatting | bytes 2097152 | tf_op jit(solution)/shard_map/reshape | solution.py:278
  55.4 35.2 %shard_map.136 = bf16[1024,512]{1,0:T(8,128)(2,1)} custom-call(bf16[1024,512]{1,0:T(8,128)(2,1)} %bitcast.24, bf16[256,16,128]{2,1,0:T(8,128)(2,1)} %reshape.73.ret_ref, s32[32]{0:T(128)} %multiply_add_fusion.target_ref, s32[832]{0:T(1024)} %reshape.74.adj_ref, s32[20]{0:T(128)} %face_ref.1, bf16[32,32]{1,0:T(8,128)(2,1)} %proj_ref.1, ...), custom_call_target="tpu_custom_call" | custom-call | tf_op jit(solution)/shard_map/pallas_call | solution.py:283
  90.6 2.3 %copy.38 = bf16[32,32,512]{2,1,0:T(8,128)(2,1)} copy(bf16[32,32,512]{2,1,0:T(8,128)(2,1)} %bitcast.21) | data formatting | bytes 2097152
  (6 shorter events, 0.0 us)
Async XLA Ops:
  0.0 24.2 %copy-start = (bf16[512,2048]{1,0:T(8,128)(2,1)S(1)}, bf16[512,2048]{1,0:T(8,128)(2,1)}, u32[]{:S(2)}) copy-start(bf16[512,2048]{1,0:T(8,128)(2,1)} %param.15) | copy-start | bytes 6291460
  27.1 8.0 %copy-start.1 = (bf16[27,32,32]{2,1,0:T(8,128)(2,1)S(1)}, bf16[27,32,32]{2,1,0:T(8,128)(2,1)}, u32[]{:S(2)}) copy-start(bf16[27,32,32]{2,1,0:T(8,128)(2,1)} %param.21) | copy-start | bytes 165892
  30.3 23.6 %all-to-all-start.1 = ((bf16[128,2,2048]{2,1,0:T(2,128)(2,1)}), bf16[128,2,2048]{2,1,0:T(2,128)(2,1)S(1)}, u32[]{:S(2)}, u32[]{:S(2)}) async-start(bf16[128,2,2048]{2,1,0:T(2,128)(2,1)} %broadcast_select_fusion.1), calls=%async_computation.1 | async-start | bytes 2097152 | tf_op jit(solution)/shard_map/all_to_all | solution.py:277
  35.0 10.3 %copy-start.2 = (s32[32,26]{1,0:T(8,128)S(1)}, s32[32,26]{1,0:T(8,128)}, u32[]{:S(2)}) copy-start(s32[32,26]{1,0:T(8,128)} %param.19) | copy-start | bytes 9988
  35.0 11.0 %copy-start.4 = (f32[32]{0:T(128)S(1)}, f32[32]{0:T(128)}, u32[]{:S(2)}) copy-start(f32[32]{0:T(128)} %param.22) | copy-start | bytes 388
  35.0 11.7 %copy-start.5 = (f32[32]{0:T(128)S(1)}, f32[32]{0:T(128)}, u32[]{:S(2)}) copy-start(f32[32]{0:T(128)} %param.24) | copy-start | bytes 388
  35.0 12.3 %copy-start.3 = (s32[32,1]{0,1:T(1,128)S(1)}, s32[32,1]{0,1:T(1,128)}, u32[]{:S(2)}) copy-start(s32[32,1]{0,1:T(1,128)} %param.16) | copy-start | bytes 388

commit v2 on v1

--- a/solution.py
+++ b/solution.py
@@ -1,5 +1,3 @@
-import functools
-
 import jax
 import jax.numpy as jnp
 import numpy as np
@@ -11,8 +9,7 @@
 F32 = jnp.float32
 BF16 = jnp.bfloat16
 NB = 32
-SLOTS = 45
-BLANK = 44
+SLOTS = 53
 MESH = pl.DeviceIdType.MESH
 
 
@@ -35,20 +32,16 @@
     return perm, np.concatenate([even, odd], 1)
 
 
-def strips_of(weights):
-    w = weights.reshape(3, 3, 3, 32, 32)[:, :, ::-1]
-    w = w.transpose(0, 1, 4, 2, 3).reshape(9, 32, 96)
-    return jnp.pad(w, ((0, 0), (0, 0), (0, 160)))
-
-
-def build_band(strip_ref, band_ref):
+def build_band(weight_ref, band_ref):
     lane = lax.broadcasted_iota(jnp.int32, (32, 256), 1)
     zero = jnp.zeros((32, 256), F32)
 
     def per_x(i, carry):
         first, last = [], []
         for j in range(3):
-            strip = strip_ref[3 * i + j].astype(F32)
+            taps = [weight_ref[9 * i + 3 * j + k].astype(F32) for k in (2, 1, 0)]
+            taps = jnp.concatenate(taps + [jnp.zeros((32, 32), F32)], axis=0)
+            strip = jnp.concatenate([taps.T, jnp.zeros((32, 128), F32)], axis=1)
             for z in range(8):
                 rolled = strip if z == 1 else pltpu.roll(strip, (32 * (z - 1)) % 256, 1)
                 if z == 0:
@@ -73,27 +66,69 @@
     return jnp.where(lane < 64, a, b)
 
 
+def wait_bytes(ref, sem):
+    pltpu.make_async_copy(ref, ref, sem).wait()
+
+
 def kernel(
-    fine_ref, ret_ref, target_ref, adj_ref, face_ref, proj_ref, perm_ref, unperm_ref, up_ref,
-    strip1_ref, bias1_ref, strip2_ref, bias2_ref, out_ref,
-    tile_ref, edge_ref, pad_ref, band1_ref, band2_ref, level_ref, par_ref, even_ref, odd_ref,
-    sum_ref, mix_ref, xs_ref, ys_ref, yrow_ref, xr_ref, yr_ref, send_sem, recv_sem,
+    owner_ref, cell_ref, face_ref, adj_ref, bias1_ref, bias2_ref, proj_ref, weight1_ref, weight2_ref,
+    fine_hbm, cache_hbm, perm_hbm, up_hbm, out_ref,
+    fine_ref, cache_ref, perm_ref, up_ref, code_ref, codes_ref, hot_ref, ans_ref, stage_ref, ret_ref, rank_ref,
+    finep_ref, tile_ref, edge_ref, pad_ref, band1_ref, band2_ref, level_ref, par_ref,
+    sum_ref, mix_ref, bias_ref, xs_ref, ys_ref, yrow_ref, xr_ref, yr_ref,
+    send_sem, recv_sem, load_sem, pair_sem, block_sem, reply_sem,
 ):
     gx, gy = lax.axis_index("gx"), lax.axis_index("gy")
     nx, ny = lax.axis_size("gx"), lax.axis_size("gy")
+    devices = nx * ny
     up_x, down_x = lax.rem(gx + 1, nx), lax.rem(gx + nx - 1, nx)
     up_y, down_y = lax.rem(gy + 1, ny), lax.rem(gy + ny - 1, ny)
     neighbours = [(up_x, gy), (down_x, gy), (gx, up_y), (gx, down_y)]
+    me = gx * ny + gy
+    chip, core = gx // 2, lax.rem(gx, 2)
+    near = 2 * ny
+    far = nx // 2
+    spot = gy * 2 + core
+
+    def near_device(k):
+        at = lax.rem(spot + k, near)
+        return (chip * 2 + lax.rem(at, 2), at // 2)
+
+    def far_device(k):
+        return (lax.rem(chip + k, far) * 2 + core, gy)
+
     barrier = pltpu.get_barrier_semaphore()
-    for other in neighbours:
-        pl.semaphore_signal(barrier, inc=1, device_id=other, device_id_type=MESH)
-    pl.semaphore_wait(barrier, 4)
-
-    build_band(strip1_ref, band1_ref)
-    build_band(strip2_ref, band2_ref)
+    for k in range(1, near):
+        pl.semaphore_signal(barrier, inc=1, device_id=near_device(k), device_id_type=MESH)
+    for k in range(1, far):
+        pl.semaphore_signal(barrier, inc=1, device_id=far_device(k), device_id_type=MESH)
+    loads = [
+        pltpu.make_async_copy(src, dst, load_sem.at[n])
+        for n, (src, dst) in enumerate(
+            [(fine_hbm, fine_ref), (cache_hbm, cache_ref), (perm_hbm, perm_ref), (up_hbm, up_ref)]
+        )
+    ]
+    for load in loads:
+        load.start()
+
+    lane = lax.broadcasted_iota(jnp.int32, (1, 128), 1)
+    code = jnp.full((1, 128), -1, jnp.int32)
+    for b in range(NB):
+        code = jnp.where(lane == b, owner_ref[b, 0] * 512 + cell_ref[b], code)
+    code_ref[0:1] = code
+    here = chip * near + spot
+    codes_ref[pl.ds(here, 1)] = code
+
+    build_band(weight1_ref, band1_ref)
     for x in range(8):
-        tile_ref[x, BLANK] = jnp.zeros((8, 256), F32)
-        edge_ref[x, BLANK] = jnp.zeros((8, 128), F32)
+        tile_ref[x, 0] = jnp.zeros((8, 256), F32)
+        edge_ref[x, 0] = jnp.zeros((8, 128), F32)
+    lane = lax.broadcasted_iota(jnp.int32, (1, 256), 1)
+    for n, ref in enumerate((bias1_ref, bias2_ref)):
+        line = jnp.zeros((1, 256), F32)
+        for o in range(32):
+            line = jnp.where(lane % 32 == o, ref[o], line)
+        bias_ref[n : n + 1] = line
 
     wide = jnp.concatenate([proj_ref[...]] * 8, axis=0)
     chan = lax.broadcasted_iota(jnp.int32, (32, 256), 0)
@@ -104,12 +139,99 @@
     lane = lax.broadcasted_iota(jnp.int32, (256, 256), 1)
     mix_ref[...] = jnp.where(row // 32 == lane % 128 // 16, spread, 0.0).astype(BF16)
 
+    pl.semaphore_wait(barrier, near + far - 2)
+
+    own_row = codes_ref.at[pl.ds(here, 1)]
+    for k in range(1, near):
+        pltpu.make_async_remote_copy(
+            src_ref=code_ref.at[pl.ds(0, 1)], dst_ref=own_row, send_sem=pair_sem.at[0], recv_sem=pair_sem.at[1],
+            device_id=near_device(k), device_id_type=MESH).start()
+
+    def ranks(b, carry):
+        count = jnp.int32(0)
+        for other in range(NB):
+            same = (owner_ref[other, 0] == owner_ref[b, 0]) & (other < b)
+            count = count + jnp.where(same, 1, 0)
+        rank_ref[b] = owner_ref[b, 0] * 2 + count
+        return carry
+
+    lax.fori_loop(0, NB, ranks, 0)
+    wait_bytes(codes_ref.at[pl.ds(0, near - 1)], pair_sem.at[0])
+    wait_bytes(codes_ref.at[pl.ds(0, near - 1)], pair_sem.at[1])
+    block = codes_ref.at[pl.ds(pl.multiple_of(chip * near, near), near)]
+    for k in range(1, far):
+        pltpu.make_async_remote_copy(
+            src_ref=block, dst_ref=block, send_sem=block_sem.at[0], recv_sem=block_sem.at[1],
+            device_id=far_device(k), device_id_type=MESH).start()
+    build_band(weight2_ref, band2_ref)
+    loads[1].wait()
+    wait_bytes(codes_ref.at[pl.ds(0, near * (far - 1))], block_sem.at[0])
+    wait_bytes(codes_ref.at[pl.ds(0, near * (far - 1))], block_sem.at[1])
+
+    codes = codes_ref[...]
+    spots = lax.broadcasted_iota(jnp.int32, codes.shape, 1).astype(F32)
+    match = (codes >> 9) == me
+    cells = (codes & 511).astype(F32)
+    lead = jnp.min(jnp.where(match, spots, 999.0), axis=1, keepdims=True)
+    one = jnp.max(jnp.where(match & (spots == lead), cells, -1.0), axis=1, keepdims=True)
+    two = jnp.max(jnp.where(match & (spots != lead), cells, -1.0), axis=1, keepdims=True)
+    index = lax.broadcasted_iota(jnp.int32, (codes.shape[0], 512), 1).astype(F32)
+    hot_ref[pl.ds(0, devices), :] = jnp.where(index == one, 1.0, 0.0).astype(BF16)
+    hot_ref[pl.ds(devices, devices), :] = jnp.where(index == two, 1.0, 0.0).astype(BF16)
+
+    def answer(n, carry):
+        cols = pl.ds(pl.multiple_of(256 * n, 256), 256)
+        rows = jnp.dot(hot_ref[...], cache_ref[:, cols], preferred_element_type=F32)
+        height = 2 * devices
+        ans_ref[pl.ds(pl.multiple_of(2 * n * height, height), height), :] = rows[:, :128]
+        ans_ref[pl.ds(pl.multiple_of((2 * n + 1) * height, height), height), :] = rows[:, 128:]
+        return carry
+
+    lax.fori_loop(0, 8, answer, 0)
+
+    def answer_to(dx, dy):
+        at = dx // 2 * near + dy * 2 + lax.rem(dx, 2)
+        first = ans_ref[pl.ds(at, 16, stride=2 * devices), :]
+        second = ans_ref[pl.ds(devices + at, 16, stride=2 * devices), :]
+        return first.astype(BF16), second.astype(BF16)
+
+    mine = answer_to(gx, gy)
+    ret_ref[2 * me] = mine[0]
+    ret_ref[2 * me + 1] = mine[1]
+
+    def reply(i, carry):
+        to = lax.rem(me + lax.rem(51 * i, devices), devices)
+        dx, dy = to // ny, lax.rem(to, ny)
+        pair = answer_to(dx, dy)
+        stage_ref[2 * to] = pair[0]
+        stage_ref[2 * to + 1] = pair[1]
+        pltpu.make_async_remote_copy(
+            src_ref=stage_ref.at[pl.ds(2 * to, 2)], dst_ref=ret_ref.at[pl.ds(2 * me, 2)],
+            send_sem=reply_sem.at[0], recv_sem=reply_sem.at[1],
+            device_id=(dx, dy), device_id_type=MESH).start()
+        return carry
+
+    lax.fori_loop(1, devices, reply, 0)
+
+    for n in (0, 2, 3):
+        loads[n].wait()
+
+    def unfold(g, carry):
+        fine = fine_ref[pl.ds(pl.multiple_of(8 * g, 8), 8)].reshape(256, 512)
+        rows = pl.ds(pl.multiple_of(256 * g, 256), 256)
+        finep_ref[rows, :] = jnp.dot(fine, perm_ref[...], preferred_element_type=F32)
+        return carry
+
+    lax.fori_loop(0, 4, unfold, 0)
+    wait_bytes(ret_ref.at[pl.ds(0, 2 * devices - 2)], reply_sem.at[0])
+    wait_bytes(ret_ref.at[pl.ds(0, 2 * devices - 2)], reply_sem.at[1])
+
     def place(x, slot, tile):
         tile_ref[x, slot] = tile
         edge_ref[x, slot] = edge_lanes(tile[:, :128], tile[:, 128:])
 
     def fetch(b, carry):
-        par_ref[pl.ds(pl.multiple_of(16 * b, 16), 16), :] = ret_ref[target_ref[b]]
+        par_ref[pl.ds(pl.multiple_of(16 * b, 16), 16), :] = ret_ref[rank_ref[b]]
         return carry
 
     lax.fori_loop(0, NB, fetch, 0)
@@ -120,8 +242,7 @@
         both = jnp.dot(pair, up_ref[...], preferred_element_type=F32).astype(BF16)
         stack = jnp.concatenate([both[:, :512], both[:, 512:]], axis=0)
         mapped = jnp.dot(mix_ref[...], stack, preferred_element_type=F32)
-        fine = jnp.dot(fine_ref[rows, :], perm_ref[...], preferred_element_type=F32)
-        rounded = (fine + mapped).astype(BF16)
+        rounded = (finep_ref[rows, :] + mapped).astype(BF16)
         level_ref[rows, :] = rounded
         wide = rounded.astype(F32)
         for n in range(8):
@@ -130,7 +251,7 @@
             turned = square.T
             for x in range(8):
                 low, high = turned[8 * x : 8 * x + 8], turned[64 + 8 * x : 72 + 8 * x]
-                place(x, 8 * g + n, jnp.concatenate([low, high], axis=1))
+                place(x, 8 * g + n + 1, jnp.concatenate([low, high], axis=1))
         return carry
 
     lax.fori_loop(0, 4, level, 0)
@@ -144,12 +265,12 @@
             x = 7 if d == 0 else 0
             for j in range(0, 8, 2):
                 two = jnp.concatenate(
-                    [tile_ref[x, face_ref[8 * d + j]], tile_ref[x, face_ref[8 * d + j + 1]]], axis=0
+                    [tile_ref[x, face_ref[8 * d + j] + 1], tile_ref[x, face_ref[8 * d + j + 1] + 1]], axis=0
                 )
                 xs_ref[turn, d, pl.ds(8 * j, 16), :] = two.astype(BF16)
             y = 7 if d == 0 else 0
             for j in range(2):
-                at = face_ref[16 + 2 * d + j]
+                at = face_ref[16 + 2 * d + j] + 1
                 for x in range(8):
                     yrow_ref[pl.ds(8 * j + x, 1), :] = tile_ref[x, at, pl.ds(y, 1), :]
             ys_ref[turn, d] = yrow_ref[...].astype(BF16)
@@ -176,13 +297,13 @@
                 if j % 2 == 0:
                     two = xr_ref[turn, d, pl.ds(8 * j, 16), :].astype(F32)
                     two = jnp.where(here, two, 0.0)
-                place(7 if d == 0 else 0, 32 + j, two[8 * (j % 2) : 8 * (j % 2) + 8])
+                place(7 if d == 0 else 0, 33 + 8 * d + j, two[8 * (j % 2) : 8 * (j % 2) + 8])
             here = (gy > 0) if d == 0 else (gy < ny - 1)
             rows = jnp.where(here, yr_ref[turn, d].astype(F32), 0.0)
             for j in range(2):
                 for x in range(8):
                     line = rows[8 * j + x : 8 * j + x + 1]
-                    place(x, 40 + 2 * d + j, jnp.broadcast_to(line, (8, 256)))
+                    place(x, 49 + 2 * d + j, jnp.broadcast_to(line, (8, 256)))
 
     def padded_tile(b, px):
         dx = -1 if px == 0 else (1 if px == 9 else 0)
@@ -190,8 +311,8 @@
 
         def at(dy, dz):
             if dx == 0 and dy == 0 and dz == 0:
-                return b
-            return adj_ref[b * 26 + column_of(dx, dy, dz)]
+                return b + 1
+            return adj_ref[b, column_of(dx, dy, dz)] + 1
 
         mid = tile_ref[x, at(0, 0)]
         low = pltpu.roll(jnp.where(row8 == 7, tile_ref[x, at(-1, 0)], mid), 1, 0)
@@ -214,21 +335,21 @@
 
         lax.fori_loop(0, NB // 2, per_pair, 0)
 
-    def conv(x, band_ref, bias_ref):
+    def conv(x, band_ref, bias):
         total = jnp.dot(pad_ref[x], band_ref[0], preferred_element_type=F32)
         total += jnp.dot(pad_ref[x + 1], band_ref[1], preferred_element_type=F32)
         total += jnp.dot(pad_ref[x + 2], band_ref[2], preferred_element_type=F32)
-        return total + bias_ref[...]
+        return total + bias_ref[pl.ds(bias, 1)]
 
     land(0, exchange(0))
     pad_all()
 
     def first(x, carry):
-        v = conv(x, band1_ref, bias1_ref)
+        v = conv(x, band1_ref, 0)
         h = (v / (1.0 + jnp.exp(-v))).astype(BF16).astype(F32)
-        tile_ref[x, pl.ds(0, NB)] = h.reshape(NB, 8, 256)
+        tile_ref[x, pl.ds(1, NB)] = h.reshape(NB, 8, 256)
         e = edge_lanes(h[:, :128], h[:, 128:])
-        edge_ref[x, pl.ds(0, NB)] = e.reshape(NB, 8, 128)
+        edge_ref[x, pl.ds(1, NB)] = e.reshape(NB, 8, 128)
         return carry
 
     lax.fori_loop(0, 8, first, 0)
@@ -236,7 +357,7 @@
     pad_all()
 
     def second(x, carry):
-        sum_ref[x] = conv(x, band2_ref, bias2_ref).reshape(NB, 8, 256)
+        sum_ref[x] = conv(x, band2_ref, 1).reshape(NB, 8, 256)
         return carry
 
     lax.fori_loop(0, 8, second, 0)
@@ -249,16 +370,10 @@
             turned = jnp.concatenate([t[:, :128] for t in tall] + [t[:, 128:] for t in tall], axis=0).T
             parts.append(jnp.concatenate([turned[32 * k : 32 * k + 32] for k in range(4)], axis=1))
         total = jnp.concatenate(parts, axis=0) + level_ref[rows, :].astype(F32)
-        out = jnp.dot(total.astype(BF16), unperm_ref[...], preferred_element_type=F32)
-        out_ref[rows, :] = out.astype(BF16)
+        out_ref[rows, :] = total.astype(BF16)
         return carry
 
     lax.fori_loop(0, 4, finish, 0)
-
-
-def lookup(cache, cells):
-    rows = jnp.take(cache, jnp.maximum(cells, 0), axis=0)
-    return jnp.where((cells >= 0)[:, None], rows, jnp.zeros_like(rows))
 
 
 def per_device(
@@ -266,26 +381,28 @@
     parent_proj, conv_first, bias_first, conv_second, bias_second,
 ):
     devices = lax.axis_size("gx") * lax.axis_size("gy")
-    owners = parent_owner[:, 0]
-    onehot = (owners[:, None] == jnp.arange(devices, dtype=jnp.int32)[None, :]).astype(jnp.int32)
-    before = jnp.cumsum(onehot, axis=0) - onehot
-    position = jnp.sum(before * onehot, axis=1)
-    target = owners * 2 + position
-    requests = jnp.full((devices * 2,), -1, jnp.int32).at[target].set(parent_cell)
-    arrived = lax.all_to_all(requests, ("gx", "gy"), split_axis=0, concat_axis=0, tiled=True)
-    answers = lookup(coarse_cache, arrived)
-    returned = lax.all_to_all(answers, ("gx", "gy"), split_axis=0, concat_axis=0, tiled=True)
-    returned = returned.reshape(devices * 2, 16, 128)
-    places = jnp.where(adjacency < 0, BLANK, jnp.where(adjacency >= 40, adjacency - 8, adjacency))
     perm, up = lane_tables()
     vmem = pl.BlockSpec(memory_space=pltpu.VMEM)
     smem = pl.BlockSpec(memory_space=pltpu.SMEM)
+    hbm = pl.BlockSpec(memory_space=pl.ANY)
     out = pl.pallas_call(
         kernel,
         out_shape=jax.ShapeDtypeStruct((NB * 32, 512), BF16),
-        in_specs=[vmem, vmem, smem, smem, smem] + [vmem] * 8,
+        in_specs=[smem] * 6 + [vmem] * 3 + [hbm] * 4,
         out_specs=vmem,
         scratch_shapes=[
+            pltpu.VMEM((NB, 32, 512), BF16),
+            pltpu.VMEM((512, 2048), BF16),
+            pltpu.VMEM((512, 512), BF16),
+            pltpu.VMEM((128, 1024), BF16),
+            pltpu.VMEM((8, 128), jnp.int32),
+            pltpu.VMEM((devices, 128), jnp.int32),
+            pltpu.VMEM((2 * devices, 512), BF16),
+            pltpu.VMEM((32 * devices, 128), F32),
+            pltpu.VMEM((2 * devices, 16, 128), BF16),
+            pltpu.VMEM((2 * devices, 16, 128), BF16),
+            pltpu.SMEM((NB,), jnp.int32),
+            pltpu.VMEM((NB * 32, 512), F32),
             pltpu.VMEM((8, SLOTS, 8, 256), F32),
             pltpu.VMEM((8, SLOTS, 8, 128), F32),
             pltpu.VMEM((10, 256, 1024), BF16),
@@ -293,10 +410,9 @@
             pltpu.VMEM((3, 1024, 256), BF16),
             pltpu.VMEM((NB * 32, 512), BF16),
             pltpu.VMEM((NB * 16, 128), BF16),
-            pltpu.VMEM((8, 128), BF16),
-            pltpu.VMEM((8, 128), BF16),
             pltpu.VMEM((8, NB, 8, 256), F32),
             pltpu.VMEM((256, 256), BF16),
+            pltpu.VMEM((8, 256), F32),
             pltpu.VMEM((2, 2, 64, 256), BF16),
             pltpu.VMEM((2, 2, 16, 256), BF16),
             pltpu.VMEM((16, 256), F32),
@@ -304,16 +420,19 @@
             pltpu.VMEM((2, 2, 16, 256), BF16),
             pltpu.SemaphoreType.DMA((2, 4)),
             pltpu.SemaphoreType.DMA((2, 4)),
+            pltpu.SemaphoreType.DMA((4,)),
+            pltpu.SemaphoreType.DMA((2,)),
+            pltpu.SemaphoreType.DMA((2,)),
+            pltpu.SemaphoreType.DMA((2,)),
         ],
         compiler_params=pltpu.CompilerParams(
             collective_id=0, has_side_effects=True, vmem_limit_bytes=56 * 1024 * 1024
         ),
     )(
-        fine_features.reshape(NB * 32, 512), returned, target, places.reshape(-1), face_list, parent_proj,
-        jnp.asarray(perm, BF16), jnp.asarray(perm.T, BF16), jnp.asarray(up, BF16),
-        strips_of(conv_first), jnp.tile(bias_first, 8)[None, :],
-        strips_of(conv_second), jnp.tile(bias_second, 8)[None, :],
+        parent_owner, parent_cell, face_list, adjacency, bias_first, bias_second, parent_proj, conv_first,
+        conv_second, fine_features, coarse_cache, jnp.asarray(perm, BF16), jnp.asarray(up, BF16),
     )
+    out = jnp.dot(out, jnp.asarray(perm.T, BF16), preferred_element_type=F32).astype(BF16)
     return out.reshape(NB, 32, 512)
 
 

time: 93.4 us -> 68.1 us (0.73)
  Pallas kernels: 35.2 us -> 63.7 us
  blocking collectives: 20.1 us -> 0 us
  local copies, waits for them, and re-layouts: 20.4 us -> 1.34 us
  other arithmetic: 6.32 us -> 0 us
  waiting for transfers between devices: 5.98 us -> 0 us
  starting transfers between devices: 4.65 us -> 0 us
  matrix products: 0 us -> 2.9 us
    pallas_call x1, Pallas kernels: 35.2 us -> 63.7 us  [per_device(): pl.pallas_call(kernel, out_shape=jax.ShapeDtypeStruct((NB * 32, 512), BF1...]
    all_to_all x1 -> x0, blocking collectives: 20.1 us -> none  [per_device(): lax.all_to_all(requests, ('gx', 'gy'), split_axis=0, concat_axis=0, tiled...]
    all_to_all x1 -> x0, waiting for transfers between devices: 5.98 us -> none  [per_device(): lax.all_to_all(answers, ('gx', 'gy'), split_axis=0, concat_axis=0, tiled=...]
    reshape x6 -> x0, local copies, waits for them, and re-layouts: 5.81 us -> none  [the longest x2 2.71 us: strips_of(): w = weights.reshape(3, 3, 3, 32, 32)[:, :, ::-1]]
    all_to_all x1 -> x0, starting transfers between devices: 4.65 us -> none  [per_device(): lax.all_to_all(answers, ('gx', 'gy'), split_axis=0, concat_axis=0, tiled=...]
    rev x2 -> x0, local copies, waits for them, and re-layouts: 4.35 us -> none  [strips_of(): w = weights.reshape(3, 3, 3, 32, 32)[:, :, ::-1]]
    select_n x3 -> x0, other arithmetic: 3.95 us -> none  [the longest x1 3.27 us: lookup(): return jnp.where((cells >= 0)[:, None], rows, jnp.zeros_like(rows))]
    dot_general x0 -> x1, matrix products: none -> 2.9 us  [per_device(): jnp.dot(out, jnp.asarray(perm.T, BF16), preferred_element_type=F32)]
  transfers between devices with their start and end apart: 1 -> 0, of which waited for: 1 -> 0; matrix products, arithmetic and copies ran while one was open for 14% -> 0% of each run, Pallas kernels for 0% -> 0%
where the time goes in v2:
time: 68.1 us; the launch traced here: 67.9 us
  Pallas kernels  63.7 us (94%)
  matrix products  2.9 us (4%)
  local copies, waits for them, and re-layouts  1.34 us (2%)
    pallas_call x1, Pallas kernels, per_device(): pl.pallas_call(kernel, out_shape=jax.ShapeDtypeStruct((NB * 32, 512), BF1...  63.7 us
    dot_general x1, matrix products, per_device(): jnp.dot(out, jnp.asarray(perm.T, BF16), preferred_element_type=F32)  2.9 us

profile of v2, /device:TPU:0, one launch (start us, length us, event | category | flops | bytes accessed | tf_op | source)
XLA Modules:
  0.0 67.9 jit_solution(6516165939192315157)
XLA Ops:
  0.0 1.3 %copy.15.owner_ref = s32[32,1]{1,0:T(8,128)} copy(s32[32,1]{0,1:T(1,128)} %param.16) | data formatting | bytes 256 | tf_op args[2]
  1.3 0.0 copy-start
  1.3 63.7 %shard_map.136 = bf16[1024,512]{1,0:T(8,128)(2,1)} custom-call(s32[32,1]{1,0:T(8,128)} %copy.15.owner_ref, s32[32]{0:T(128)} %cell_ref.1, s32[20]{0:T(128)} %face_ref.1, s32[32,26]{1,0:T(8,128)} %adj_ref.1, f32[32]{0:T(128)} %bias1_ref.1, f32[32]{0:T(128)} %bias2_ref.1, bf16[32,32]{1,0:T(8,128)(2,1)} %proj_ref.1, bf16[27,32,32]{2,1,0:T(8,128)(2,1)} %weight1_ref.1, ...), custom_call_target="tpu_custom_call" | custom-call | tf_op jit(solution)/shard_map/pallas_call | solution.py:388
  65.0 0.0 copy-done
  65.0 2.9 %convolution_convert_fusion = bf16[1024,512]{1,0:T(8,128)(2,1)} fusion(bf16[1024,512]{1,0:T(8,128)(2,1)} %shard_map.136, bf16[512,512]{1,0:T(8,128)(2,1)S(1)} %copy-done), kind=kOutput, calls=%fused_computation | convolution fusion | flops 537395200 | bytes 2621440 | tf_op jit(solution)/shard_map/dot_general | solution.py:435
Async XLA Ops:
  1.3 63.7 %copy-start = (bf16[512,512]{1,0:T(8,128)(2,1)S(1)}, bf16[512,512]{1,0:T(8,128)(2,1)}, u32[]{:S(2)}) copy-start(bf16[512,512]{1,0:T(8,128)(2,1)} %constant.8.clone) | copy-start | bytes 1572868

commit v3 on v2

--- a/solution.py
+++ b/solution.py
@@ -11,6 +11,7 @@
 NB = 32
 SLOTS = 53
 MESH = pl.DeviceIdType.MESH
+GROUPS = [[0, 1, 6, 7, 2, 3], [4, 5]]
 
 
 def column_of(dx, dy, dz):
@@ -114,30 +115,10 @@
     lane = lax.broadcasted_iota(jnp.int32, (1, 128), 1)
     code = jnp.full((1, 128), -1, jnp.int32)
     for b in range(NB):
-        code = jnp.where(lane == b, owner_ref[b, 0] * 512 + cell_ref[b], code)
+        code = jnp.where(lane == b, owner_ref[b] * 512 + cell_ref[b], code)
     code_ref[0:1] = code
     here = chip * near + spot
     codes_ref[pl.ds(here, 1)] = code
-
-    build_band(weight1_ref, band1_ref)
-    for x in range(8):
-        tile_ref[x, 0] = jnp.zeros((8, 256), F32)
-        edge_ref[x, 0] = jnp.zeros((8, 128), F32)
-    lane = lax.broadcasted_iota(jnp.int32, (1, 256), 1)
-    for n, ref in enumerate((bias1_ref, bias2_ref)):
-        line = jnp.zeros((1, 256), F32)
-        for o in range(32):
-            line = jnp.where(lane % 32 == o, ref[o], line)
-        bias_ref[n : n + 1] = line
-
-    wide = jnp.concatenate([proj_ref[...]] * 8, axis=0)
-    chan = lax.broadcasted_iota(jnp.int32, (32, 256), 0)
-    lane = lax.broadcasted_iota(jnp.int32, (32, 256), 1)
-    pick = jnp.where(chan == 2 * (lane % 16) + lane // 128, 1.0, 0.0).astype(BF16)
-    spread = jnp.dot(wide, pick, preferred_element_type=F32)
-    row = lax.broadcasted_iota(jnp.int32, (256, 256), 0)
-    lane = lax.broadcasted_iota(jnp.int32, (256, 256), 1)
-    mix_ref[...] = jnp.where(row // 32 == lane % 128 // 16, spread, 0.0).astype(BF16)
 
     pl.semaphore_wait(barrier, near + far - 2)
 
@@ -147,15 +128,6 @@
             src_ref=code_ref.at[pl.ds(0, 1)], dst_ref=own_row, send_sem=pair_sem.at[0], recv_sem=pair_sem.at[1],
             device_id=near_device(k), device_id_type=MESH).start()
 
-    def ranks(b, carry):
-        count = jnp.int32(0)
-        for other in range(NB):
-            same = (owner_ref[other, 0] == owner_ref[b, 0]) & (other < b)
-            count = count + jnp.where(same, 1, 0)
-        rank_ref[b] = owner_ref[b, 0] * 2 + count
-        return carry
-
-    lax.fori_loop(0, NB, ranks, 0)
     wait_bytes(codes_ref.at[pl.ds(0, near - 1)], pair_sem.at[0])
     wait_bytes(codes_ref.at[pl.ds(0, near - 1)], pair_sem.at[1])
     block = codes_ref.at[pl.ds(pl.multiple_of(chip * near, near), near)]
@@ -163,7 +135,6 @@
         pltpu.make_async_remote_copy(
             src_ref=block, dst_ref=block, send_sem=block_sem.at[0], recv_sem=block_sem.at[1],
             device_id=far_device(k), device_id_type=MESH).start()
-    build_band(weight2_ref, band2_ref)
     loads[1].wait()
     wait_bytes(codes_ref.at[pl.ds(0, near * (far - 1))], block_sem.at[0])
     wait_bytes(codes_ref.at[pl.ds(0, near * (far - 1))], block_sem.at[1])
@@ -212,6 +183,37 @@
         return carry
 
     lax.fori_loop(1, devices, reply, 0)
+
+    def ranks(b, carry):
+        count = jnp.int32(0)
+        for other in range(NB):
+            same = (owner_ref[other] == owner_ref[b]) & (other < b)
+            count = count + jnp.where(same, 1, 0)
+        rank_ref[b] = owner_ref[b] * 2 + count
+        return carry
+
+    lax.fori_loop(0, NB, ranks, 0)
+    build_band(weight1_ref, band1_ref)
+    build_band(weight2_ref, band2_ref)
+    yrow_ref[...] = jnp.zeros_like(yrow_ref)
+    for x in range(8):
+        tile_ref[x, 0] = jnp.zeros((8, 256), F32)
+        edge_ref[x, 0] = jnp.zeros((8, 128), F32)
+    lane = lax.broadcasted_iota(jnp.int32, (1, 256), 1)
+    for n, ref in enumerate((bias1_ref, bias2_ref)):
+        line = jnp.zeros((1, 256), F32)
+        for o in range(32):
+            line = jnp.where(lane % 32 == o, ref[o], line)
+        bias_ref[n : n + 1] = line
+
+    wide = jnp.concatenate([proj_ref[...]] * 8, axis=0)
+    chan = lax.broadcasted_iota(jnp.int32, (32, 256), 0)
+    lane = lax.broadcasted_iota(jnp.int32, (32, 256), 1)
+    pick = jnp.where(chan == 2 * (lane % 16) + lane // 128, 1.0, 0.0).astype(BF16)
+    spread = jnp.dot(wide, pick, preferred_element_type=F32)
+    row = lax.broadcasted_iota(jnp.int32, (256, 256), 0)
+    lane = lax.broadcasted_iota(jnp.int32, (256, 256), 1)
+    mix_ref[...] = jnp.where(row // 32 == lane % 128 // 16, spread, 0.0).astype(BF16)
 
     for n in (0, 2, 3):
         loads[n].wait()
@@ -260,49 +262,58 @@
     row8e = lax.broadcasted_iota(jnp.int32, (8, 128), 0)
     lane8e = lax.broadcasted_iota(jnp.int32, (8, 128), 1)
 
-    def exchange(turn):
-        for d in range(2):
+    def copy_of(turn, src, dst, kind, other):
+        return pltpu.make_async_remote_copy(
+            src_ref=src, dst_ref=dst, send_sem=send_sem.at[turn, kind], recv_sem=recv_sem.at[turn, kind],
+            device_id=neighbours[other], device_id_type=MESH)
+
+    def x_copies(turn):
+        return [copy_of(turn, xs_ref.at[turn, d], xr_ref.at[turn, d], d, d) for d in range(2)]
+
+    def y_copies(turn, group):
+        return [
+            copy_of(turn, ys_ref.at[turn, d, group], yr_ref.at[turn, d, group], 2 + 2 * d + group, 2 + d)
+            for d in range(2)
+        ]
+
+    def send_x(turn):
+        for d, copy in enumerate(x_copies(turn)):
             x = 7 if d == 0 else 0
             for j in range(0, 8, 2):
                 two = jnp.concatenate(
                     [tile_ref[x, face_ref[8 * d + j] + 1], tile_ref[x, face_ref[8 * d + j + 1] + 1]], axis=0
                 )
                 xs_ref[turn, d, pl.ds(8 * j, 16), :] = two.astype(BF16)
+            copy.start()
+
+    def send_y(turn, group):
+        for d, copy in enumerate(y_copies(turn, group)):
             y = 7 if d == 0 else 0
             for j in range(2):
                 at = face_ref[16 + 2 * d + j] + 1
-                for x in range(8):
-                    yrow_ref[pl.ds(8 * j + x, 1), :] = tile_ref[x, at, pl.ds(y, 1), :]
-            ys_ref[turn, d] = yrow_ref[...].astype(BF16)
-        copies = []
-        for d in range(2):
-            copies.append(pltpu.make_async_remote_copy(
-                src_ref=xs_ref.at[turn, d], dst_ref=xr_ref.at[turn, d],
-                send_sem=send_sem.at[turn, d], recv_sem=recv_sem.at[turn, d],
-                device_id=neighbours[d], device_id_type=MESH))
-            copies.append(pltpu.make_async_remote_copy(
-                src_ref=ys_ref.at[turn, d], dst_ref=yr_ref.at[turn, d],
-                send_sem=send_sem.at[turn, 2 + d], recv_sem=recv_sem.at[turn, 2 + d],
-                device_id=neighbours[2 + d], device_id_type=MESH))
-        for copy in copies:
+                for n, x in enumerate(GROUPS[group]):
+                    yrow_ref[pl.ds(8 * j + n, 1), :] = tile_ref[x, at, pl.ds(y, 1), :]
+            ys_ref[turn, d, group] = yrow_ref[...].astype(BF16)
             copy.start()
-        return copies
-
-    def land(turn, copies):
-        for copy in copies:
+
+    def land_x(turn):
+        for d, copy in enumerate(x_copies(turn)):
             copy.wait()
-        for d in range(2):
             here = (gx > 0) if d == 0 else (gx < nx - 1)
             for j in range(8):
                 if j % 2 == 0:
                     two = xr_ref[turn, d, pl.ds(8 * j, 16), :].astype(F32)
                     two = jnp.where(here, two, 0.0)
                 place(7 if d == 0 else 0, 33 + 8 * d + j, two[8 * (j % 2) : 8 * (j % 2) + 8])
+
+    def land_y(turn, group):
+        for d, copy in enumerate(y_copies(turn, group)):
+            copy.wait()
             here = (gy > 0) if d == 0 else (gy < ny - 1)
-            rows = jnp.where(here, yr_ref[turn, d].astype(F32), 0.0)
+            rows = jnp.where(here, yr_ref[turn, d, group].astype(F32), 0.0)
             for j in range(2):
-                for x in range(8):
-                    line = rows[8 * j + x : 8 * j + x + 1]
+                for n, x in enumerate(GROUPS[group]):
+                    line = rows[8 * j + n : 8 * j + n + 1]
                     place(x, 49 + 2 * d + j, jnp.broadcast_to(line, (8, 256)))
 
     def padded_tile(b, px):
@@ -326,41 +337,58 @@
         emid = jnp.where((lane8e >= 32) & (lane8e < 96), ends[1], elow)
         return jnp.concatenate([low, mid, high, emid, ehigh], axis=1)
 
-    def pad_all():
+    def pad_planes(planes):
         def per_pair(n, carry):
-            for px in range(10):
+            for px in planes:
                 two = jnp.concatenate([padded_tile(2 * n, px), padded_tile(2 * n + 1, px)], axis=0)
                 pad_ref[px, pl.ds(pl.multiple_of(16 * n, 16), 16), :] = two.astype(BF16)
             return carry
 
         lax.fori_loop(0, NB // 2, per_pair, 0)
 
-    def conv(x, band_ref, bias):
-        total = jnp.dot(pad_ref[x], band_ref[0], preferred_element_type=F32)
-        total += jnp.dot(pad_ref[x + 1], band_ref[1], preferred_element_type=F32)
-        total += jnp.dot(pad_ref[x + 2], band_ref[2], preferred_element_type=F32)
-        return total + bias_ref[pl.ds(bias, 1)]
-
-    land(0, exchange(0))
-    pad_all()
-
-    def first(x, carry):
-        v = conv(x, band1_ref, 0)
+    def land_and_pad(turn):
+        land_x(turn)
+        land_y(turn, 0)
+        pad_planes([0, 9] + [x + 1 for x in GROUPS[0]])
+        land_y(turn, 1)
+        pad_planes([x + 1 for x in GROUPS[1]])
+
+    def conv(pair, band_ref, bias):
+        total = bias_ref[pl.ds(bias, 1)]
+        for i in range(3):
+            rows = pad_ref[pl.ds(2 * pair + i, 2)].reshape(512, 1024)
+            total = total + jnp.dot(rows, band_ref[i], preferred_element_type=F32)
+        return total
+
+    send_x(0)
+    send_y(0, 0)
+    send_y(0, 1)
+    land_and_pad(0)
+
+    def first(pair):
+        v = conv(pair, band1_ref, 0)
         h = (v / (1.0 + jnp.exp(-v))).astype(BF16).astype(F32)
-        tile_ref[x, pl.ds(1, NB)] = h.reshape(NB, 8, 256)
+        tile_ref[pl.ds(2 * pair, 2), pl.ds(1, NB)] = h.reshape(2, NB, 8, 256)
         e = edge_lanes(h[:, :128], h[:, 128:])
-        edge_ref[x, pl.ds(1, NB)] = e.reshape(NB, 8, 128)
-        return carry
-
-    lax.fori_loop(0, 8, first, 0)
-    land(1, exchange(1))
-    pad_all()
-
-    def second(x, carry):
-        sum_ref[x] = conv(x, band2_ref, 1).reshape(NB, 8, 256)
-        return carry
-
-    lax.fori_loop(0, 8, second, 0)
+        edge_ref[pl.ds(2 * pair, 2), pl.ds(1, NB)] = e.reshape(2, NB, 8, 128)
+
+    def outer(n, carry):
+        first(3 * n)
+        return carry
+
+    lax.fori_loop(0, 2, outer, 0)
+    send_x(1)
+    first(1)
+    send_y(1, 0)
+    first(2)
+    send_y(1, 1)
+    land_and_pad(1)
+
+    def second(pair, carry):
+        sum_ref[pl.ds(2 * pair, 2)] = conv(pair, band2_ref, 1).reshape(2, NB, 8, 256)
+        return carry
+
+    lax.fori_loop(0, 4, second, 0)
 
     def finish(g, carry):
         rows = pl.ds(pl.multiple_of(256 * g, 256), 256)
@@ -374,6 +402,16 @@
         return carry
 
     lax.fori_loop(0, 4, finish, 0)
+
+
+def reorder(values_ref, perm_ref, out_ref):
+    def part(g, carry):
+        rows = values_ref[pl.ds(pl.multiple_of(256 * g, 256), 256)]
+        rows = jnp.dot(rows, perm_ref[...], preferred_element_type=F32).astype(BF16)
+        out_ref[pl.ds(8 * g, 8)] = rows.reshape(8, 32, 512)
+        return carry
+
+    lax.fori_loop(0, 4, part, 0)
 
 
 def per_device(
@@ -414,12 +452,12 @@
             pltpu.VMEM((256, 256), BF16),
             pltpu.VMEM((8, 256), F32),
             pltpu.VMEM((2, 2, 64, 256), BF16),
-            pltpu.VMEM((2, 2, 16, 256), BF16),
+            pltpu.VMEM((2, 2, 2, 16, 256), BF16),
             pltpu.VMEM((16, 256), F32),
             pltpu.VMEM((2, 2, 64, 256), BF16),
-            pltpu.VMEM((2, 2, 16, 256), BF16),
-            pltpu.SemaphoreType.DMA((2, 4)),
-            pltpu.SemaphoreType.DMA((2, 4)),
+            pltpu.VMEM((2, 2, 2, 16, 256), BF16),
+            pltpu.SemaphoreType.DMA((2, 6)),
+            pltpu.SemaphoreType.DMA((2, 6)),
             pltpu.SemaphoreType.DMA((4,)),
             pltpu.SemaphoreType.DMA((2,)),
             pltpu.SemaphoreType.DMA((2,)),
@@ -429,11 +467,15 @@
             collective_id=0, has_side_effects=True, vmem_limit_bytes=56 * 1024 * 1024
         ),
     )(
-        parent_owner, parent_cell, face_list, adjacency, bias_first, bias_second, parent_proj, conv_first,
+        parent_owner.reshape(NB), parent_cell, face_list, adjacency, bias_first, bias_second, parent_proj, conv_first,
         conv_second, fine_features, coarse_cache, jnp.asarray(perm, BF16), jnp.asarray(up, BF16),
     )
-    out = jnp.dot(out, jnp.asarray(perm.T, BF16), preferred_element_type=F32).astype(BF16)
-    return out.reshape(NB, 32, 512)
+    return pl.pallas_call(
+        reorder,
+        out_shape=jax.ShapeDtypeStruct((NB, 32, 512), BF16),
+        in_specs=[vmem] * 2,
+        out_specs=vmem,
+    )(out, jnp.asarray(perm.T, BF16))
 
 
 def solution(mesh):

time: 68.1 us -> 63.7 us (0.935)
  matrix products: 2.9 us -> 0 us
  local copies, waits for them, and re-layouts: 1.34 us -> 0 us
    pallas_call x1, Pallas kernels: 63.7 us -> 60 us  [per_device(): pl.pallas_call(kernel, out_shape=jax.ShapeDtypeStruct((NB * 32, 512), BF1...]
    pallas_call x0 -> x1, Pallas kernels: none -> 3.54 us  [per_device(): pl.pallas_call(reorder, out_shape=jax.ShapeDtypeStruct((NB, 32, 512), BF1...]
    dot_general x1 -> x0, matrix products: 2.9 us -> none  [per_device(): jnp.dot(out, jnp.asarray(perm.T, BF16), preferred_element_type=F32)]
    unnamed x3 -> x0, local copies, waits for them, and re-layouts: 1.34 us -> none
where the time goes in v3:
time: 63.7 us; the launch traced here: 63.5 us
  Pallas kernels  63.5 us (100%)
    pallas_call x1, Pallas kernels, per_device(): pl.pallas_call(kernel, out_shape=jax.ShapeDtypeStruct((NB * 32, 512), BF1...  60 us
    pallas_call x1, Pallas kernels, per_device(): pl.pallas_call(reorder, out_shape=jax.ShapeDtypeStruct((NB, 32, 512), BF1...  3.54 us

profile of v3, /device:TPU:0, one launch (start us, length us, event | category | flops | bytes accessed | tf_op | source)
XLA Modules:
  0.0 63.5 jit_solution(2763083927405901597)
XLA Ops:
  0.0 60.0 %shard_map.136.values_ref = bf16[1024,512]{1,0:T(8,128)(2,1)} custom-call(s32[32]{0:T(128)} %bitcast.1, s32[32]{0:T(128)} %cell_ref.1, s32[20]{0:T(128)} %face_ref.1, s32[32,26]{1,0:T(8,128)} %adj_ref.1, f32[32]{0:T(128)} %bias1_ref.1, f32[32]{0:T(128)} %bias2_ref.1, bf16[32,32]{1,0:T(8,128)(2,1)} %proj_ref.1, bf16[27,32,32]{2,1,0:T(8,128)(2,1)} %weight1_ref.1, ...), custom_call_target="tpu_custom_call" | custom-call | tf_op jit(solution)/shard_map/pallas_call | solution.py:426
  60.0 3.5 %shard_map.137 = bf16[32,32,512]{2,1,0:T(8,128)(2,1)} custom-call(bf16[1024,512]{1,0:T(8,128)(2,1)} %shard_map.136.values_ref, bf16[512,512]{1,0:T(8,128)(2,1)} %constant.8.clone.perm_ref), custom_call_target="tpu_custom_call" | custom-call | tf_op jit(solution)/shard_map/pallas_call | solution.py:473

commit v4 on v3

--- a/solution.py
+++ b/solution.py
@@ -31,6 +31,20 @@
     even = np.concatenate([up, blank], 0)
     odd = np.concatenate([blank, up], 0)
     return perm, np.concatenate([even, odd], 1)
+
+
+def face_tables():
+    lane = np.arange(128)
+    fixed, z, free = np.where(lane < 64, 7, 0), lane % 64 // 8, lane % 8
+    picks, ups = [], []
+    for x, y in ((fixed, free), (free, fixed)):
+        voxel = 64 * x + 8 * y + z
+        cell = 16 * (x // 2) + 4 * (y // 2) + z // 2
+        picks.append((np.arange(512)[:, None] == voxel[None, :]).astype(np.float32))
+        up = (np.arange(64)[:, None] == cell[None, :]).astype(np.float32)
+        blank = np.zeros_like(up)
+        ups.append(np.concatenate([np.concatenate([up, blank], 0), np.concatenate([blank, up], 0)], 1))
+    return np.stack(picks), np.stack(ups)
 
 
 def build_band(weight_ref, band_ref):
@@ -72,12 +86,13 @@
 
 
 def kernel(
+    owner_hbm, cell_hbm, face_hbm, adj_hbm, bias1_hbm, bias2_hbm, proj_hbm, weight1_hbm, weight2_hbm,
+    fine_hbm, cache_hbm, perm_hbm, unperm_hbm, up_hbm, pick_hbm, pickup_hbm, out_hbm,
     owner_ref, cell_ref, face_ref, adj_ref, bias1_ref, bias2_ref, proj_ref, weight1_ref, weight2_ref,
-    fine_hbm, cache_hbm, perm_hbm, up_hbm, out_ref,
-    fine_ref, cache_ref, perm_ref, up_ref, code_ref, codes_ref, hot_ref, ans_ref, stage_ref, ret_ref, rank_ref,
-    finep_ref, tile_ref, edge_ref, pad_ref, band1_ref, band2_ref, level_ref, par_ref,
-    sum_ref, mix_ref, bias_ref, xs_ref, ys_ref, yrow_ref, xr_ref, yr_ref,
-    send_sem, recv_sem, load_sem, pair_sem, block_sem, reply_sem,
+    fine_ref, cache_ref, perm_ref, unperm_ref, up_ref, pick_ref, pickup_ref, code_ref, codes_ref, hot_ref, ans_ref, stage_ref, ret_ref, rank_ref,
+    finep_ref, side_ref, sidep_ref, tile_ref, edge_ref, pad_ref, band1_ref, band2_ref, level_ref, par_ref,
+    sum_ref, mix_ref, bias_ref, xs_ref, ys_ref, yrow_ref, row_ref, xr_ref, yr_ref,
+    send_sem, recv_sem, load_sem, out_sem, pair_sem, block_sem, reply_sem,
 ):
     gx, gy = lax.axis_index("gx"), lax.axis_index("gy")
     nx, ny = lax.axis_size("gx"), lax.axis_size("gy")
@@ -103,14 +118,17 @@
         pl.semaphore_signal(barrier, inc=1, device_id=near_device(k), device_id_type=MESH)
     for k in range(1, far):
         pl.semaphore_signal(barrier, inc=1, device_id=far_device(k), device_id_type=MESH)
-    loads = [
-        pltpu.make_async_copy(src, dst, load_sem.at[n])
-        for n, (src, dst) in enumerate(
-            [(fine_hbm, fine_ref), (cache_hbm, cache_ref), (perm_hbm, perm_ref), (up_hbm, up_ref)]
-        )
+    pairs = [
+        (owner_hbm, owner_ref), (cell_hbm, cell_ref), (cache_hbm, cache_ref), (face_hbm, face_ref),
+        (adj_hbm, adj_ref), (bias1_hbm, bias1_ref), (bias2_hbm, bias2_ref), (proj_hbm, proj_ref),
+        (weight1_hbm, weight1_ref), (weight2_hbm, weight2_ref), (fine_hbm, fine_ref), (perm_hbm, perm_ref),
+        (unperm_hbm, unperm_ref), (up_hbm, up_ref), (pick_hbm, pick_ref), (pickup_hbm, pickup_ref),
     ]
+    loads = [pltpu.make_async_copy(src, dst, load_sem.at[n]) for n, (src, dst) in enumerate(pairs)]
     for load in loads:
         load.start()
+    loads[0].wait()
+    loads[1].wait()
 
     lane = lax.broadcasted_iota(jnp.int32, (1, 128), 1)
     code = jnp.full((1, 128), -1, jnp.int32)
@@ -128,61 +146,68 @@
             src_ref=code_ref.at[pl.ds(0, 1)], dst_ref=own_row, send_sem=pair_sem.at[0], recv_sem=pair_sem.at[1],
             device_id=near_device(k), device_id_type=MESH).start()
 
-    wait_bytes(codes_ref.at[pl.ds(0, near - 1)], pair_sem.at[0])
     wait_bytes(codes_ref.at[pl.ds(0, near - 1)], pair_sem.at[1])
     block = codes_ref.at[pl.ds(pl.multiple_of(chip * near, near), near)]
     for k in range(1, far):
         pltpu.make_async_remote_copy(
             src_ref=block, dst_ref=block, send_sem=block_sem.at[0], recv_sem=block_sem.at[1],
             device_id=far_device(k), device_id_type=MESH).start()
-    loads[1].wait()
-    wait_bytes(codes_ref.at[pl.ds(0, near * (far - 1))], block_sem.at[0])
+    loads[2].wait()
     wait_bytes(codes_ref.at[pl.ds(0, near * (far - 1))], block_sem.at[1])
 
-    codes = codes_ref[...]
-    spots = lax.broadcasted_iota(jnp.int32, codes.shape, 1).astype(F32)
-    match = (codes >> 9) == me
-    cells = (codes & 511).astype(F32)
-    lead = jnp.min(jnp.where(match, spots, 999.0), axis=1, keepdims=True)
-    one = jnp.max(jnp.where(match & (spots == lead), cells, -1.0), axis=1, keepdims=True)
-    two = jnp.max(jnp.where(match & (spots != lead), cells, -1.0), axis=1, keepdims=True)
-    index = lax.broadcasted_iota(jnp.int32, (codes.shape[0], 512), 1).astype(F32)
-    hot_ref[pl.ds(0, devices), :] = jnp.where(index == one, 1.0, 0.0).astype(BF16)
-    hot_ref[pl.ds(devices, devices), :] = jnp.where(index == two, 1.0, 0.0).astype(BF16)
-
-    def answer(n, carry):
-        cols = pl.ds(pl.multiple_of(256 * n, 256), 256)
-        rows = jnp.dot(hot_ref[...], cache_ref[:, cols], preferred_element_type=F32)
-        height = 2 * devices
-        ans_ref[pl.ds(pl.multiple_of(2 * n * height, height), height), :] = rows[:, :128]
-        ans_ref[pl.ds(pl.multiple_of((2 * n + 1) * height, height), height), :] = rows[:, 128:]
-        return carry
-
-    lax.fori_loop(0, 8, answer, 0)
-
-    def answer_to(dx, dy):
-        at = dx // 2 * near + dy * 2 + lax.rem(dx, 2)
-        first = ans_ref[pl.ds(at, 16, stride=2 * devices), :]
-        second = ans_ref[pl.ds(devices + at, 16, stride=2 * devices), :]
-        return first.astype(BF16), second.astype(BF16)
-
-    mine = answer_to(gx, gy)
-    ret_ref[2 * me] = mine[0]
-    ret_ref[2 * me + 1] = mine[1]
-
-    def reply(i, carry):
-        to = lax.rem(me + lax.rem(51 * i, devices), devices)
-        dx, dy = to // ny, lax.rem(to, ny)
-        pair = answer_to(dx, dy)
-        stage_ref[2 * to] = pair[0]
-        stage_ref[2 * to + 1] = pair[1]
-        pltpu.make_async_remote_copy(
-            src_ref=stage_ref.at[pl.ds(2 * to, 2)], dst_ref=ret_ref.at[pl.ds(2 * me, 2)],
-            send_sem=reply_sem.at[0], recv_sem=reply_sem.at[1],
-            device_id=(dx, dy), device_id_type=MESH).start()
-        return carry
-
-    lax.fori_loop(1, devices, reply, 0)
+    half = devices // 2
+    index = lax.broadcasted_iota(jnp.int32, (half, 512), 1).astype(F32)
+
+    def answers(turn, its_core, start):
+        codes = codes_ref[pl.ds(its_core, half, stride=2), :]
+        spots = lax.broadcasted_iota(jnp.int32, codes.shape, 1).astype(F32)
+        match = (codes >> 9) == me
+        cells = (codes & 511).astype(F32)
+        lead = jnp.min(jnp.where(match, spots, 999.0), axis=1, keepdims=True)
+        one = jnp.max(jnp.where(match & (spots == lead), cells, -1.0), axis=1, keepdims=True)
+        two = jnp.max(jnp.where(match & (spots != lead), cells, -1.0), axis=1, keepdims=True)
+        hot_ref[turn, pl.ds(0, half), :] = jnp.where(index == one, 1.0, 0.0).astype(BF16)
+        hot_ref[turn, pl.ds(half, half), :] = jnp.where(index == two, 1.0, 0.0).astype(BF16)
+
+        def answer(n, carry):
+            cols = pl.ds(pl.multiple_of(256 * n, 256), 256)
+            rows = jnp.dot(hot_ref[turn], cache_ref[:, cols], preferred_element_type=F32)
+            ans_ref[turn, pl.ds(pl.multiple_of(2 * n * devices, devices), devices), :] = rows[:, :128]
+            ans_ref[turn, pl.ds(pl.multiple_of((2 * n + 1) * devices, devices), devices), :] = rows[:, 128:]
+            return carry
+
+        lax.fori_loop(0, 8, answer, 0)
+
+        def answer_to(at):
+            first = ans_ref[turn, pl.ds(at, 16, stride=devices), :]
+            second = ans_ref[turn, pl.ds(half + at, 16, stride=devices), :]
+            return first.astype(BF16), second.astype(BF16)
+
+        if turn == 0:
+            mine = answer_to(chip * ny + gy)
+            ret_ref[2 * me] = mine[0]
+            ret_ref[2 * me + 1] = mine[1]
+
+        def reply(i, carry):
+            at = lax.rem(chip * ny + gy + 27 * i, half)
+            dx, dy = at // ny * 2 + its_core, lax.rem(at, ny)
+            to = dx * ny + dy
+            pair = answer_to(at)
+            stage_ref[2 * to] = pair[0]
+            stage_ref[2 * to + 1] = pair[1]
+            pltpu.make_async_remote_copy(
+                src_ref=stage_ref.at[pl.ds(2 * to, 2)], dst_ref=ret_ref.at[pl.ds(2 * me, 2)],
+                send_sem=reply_sem.at[0], recv_sem=reply_sem.at[1],
+                device_id=(dx, dy), device_id_type=MESH).start()
+            return carry
+
+        lax.fori_loop(start, half, reply, 0)
+
+    answers(0, core, 1)
+    answers(1, 1 - core, 0)
+
+    for load in loads[3:]:
+        load.wait()
 
     def ranks(b, carry):
         count = jnp.int32(0)
@@ -196,6 +221,7 @@
     build_band(weight1_ref, band1_ref)
     build_band(weight2_ref, band2_ref)
     yrow_ref[...] = jnp.zeros_like(yrow_ref)
+    row_ref[...] = jnp.zeros_like(row_ref)
     for x in range(8):
         tile_ref[x, 0] = jnp.zeros((8, 256), F32)
         edge_ref[x, 0] = jnp.zeros((8, 128), F32)
@@ -215,9 +241,6 @@
     lane = lax.broadcasted_iota(jnp.int32, (256, 256), 1)
     mix_ref[...] = jnp.where(row // 32 == lane % 128 // 16, spread, 0.0).astype(BF16)
 
-    for n in (0, 2, 3):
-        loads[n].wait()
-
     def unfold(g, carry):
         fine = fine_ref[pl.ds(pl.multiple_of(8 * g, 8), 8)].reshape(256, 512)
         rows = pl.ds(pl.multiple_of(256 * g, 256), 256)
@@ -225,12 +248,68 @@
         return carry
 
     lax.fori_loop(0, 4, unfold, 0)
-    wait_bytes(ret_ref.at[pl.ds(0, 2 * devices - 2)], reply_sem.at[0])
+
+    def listed(group, n):
+        return face_ref[8 * group + n] if group < 2 else face_ref[16 + n % 4]
+
+    for group in range(3):
+        for n in range(8):
+            side_ref[group, n] = fine_ref[listed(group, n)]
+        sidep_ref[group] = jnp.dot(
+            side_ref[group].reshape(256, 512), pick_ref[group // 2], preferred_element_type=F32
+        )
     wait_bytes(ret_ref.at[pl.ds(0, 2 * devices - 2)], reply_sem.at[1])
 
     def place(x, slot, tile):
         tile_ref[x, slot] = tile
         edge_ref[x, slot] = edge_lanes(tile[:, :128], tile[:, 128:])
+
+    def copy_of(turn, src, dst, kind, other):
+        return pltpu.make_async_remote_copy(
+            src_ref=src, dst_ref=dst, send_sem=send_sem.at[turn, kind], recv_sem=recv_sem.at[turn, kind],
+            device_id=neighbours[other], device_id_type=MESH)
+
+    def x_copies(turn):
+        return [copy_of(turn, xs_ref.at[turn, d], xr_ref.at[turn, d], d, d) for d in range(2)]
+
+    def y_copies(turn, group):
+        return [
+            copy_of(turn, ys_ref.at[turn, d, group], yr_ref.at[turn, d, group], 2 + 2 * d + group, 2 + d)
+            for d in range(2)
+        ]
+
+    def side_tiles(group):
+        pair = jnp.concatenate([ret_ref[rank_ref[listed(group, n)]] for n in range(8)], axis=0)
+        both = jnp.dot(pair, pickup_ref[group // 2], preferred_element_type=F32).astype(BF16)
+        stack = jnp.concatenate([both[:, :128], both[:, 128:]], axis=0)
+        mapped = jnp.dot(mix_ref[...], stack, preferred_element_type=F32)
+        level = (sidep_ref[group] + mapped).astype(BF16).astype(F32)
+        turned = [level[:128].T, level[128:].T]
+        tiles = []
+        for n in range(8 if group < 2 else 4):
+            side = 64 * (group if group < 2 else n // 2)
+            source = turned[n // 4]
+            tiles.append(jnp.concatenate(
+                [source[side + 8 * z : side + 8 * z + 8, 32 * (n % 4) : 32 * (n % 4) + 32] for z in range(8)], axis=1
+            ))
+        return tiles
+
+    for d in range(2):
+        xs_ref[0, d] = jnp.concatenate(side_tiles(d), axis=0).astype(BF16)
+    for d, copy in enumerate(x_copies(0)):
+        copy.start()
+    lines = side_tiles(2)
+    for d in range(2):
+        for j in range(2):
+            yrow_ref[pl.ds(8 * j, 8), :] = lines[2 * d + j]
+        for group in range(2):
+            for j in range(2):
+                for n, x in enumerate(GROUPS[group]):
+                    row_ref[pl.ds(8 * j + n, 1), :] = yrow_ref[pl.ds(8 * j + x, 1), :]
+            ys_ref[0, d, group] = row_ref[...].astype(BF16)
+    for group in range(2):
+        for copy in y_copies(0, group):
+            copy.start()
 
     def fetch(b, carry):
         par_ref[pl.ds(pl.multiple_of(16 * b, 16), 16), :] = ret_ref[rank_ref[b]]
@@ -262,20 +341,6 @@
     row8e = lax.broadcasted_iota(jnp.int32, (8, 128), 0)
     lane8e = lax.broadcasted_iota(jnp.int32, (8, 128), 1)
 
-    def copy_of(turn, src, dst, kind, other):
-        return pltpu.make_async_remote_copy(
-            src_ref=src, dst_ref=dst, send_sem=send_sem.at[turn, kind], recv_sem=recv_sem.at[turn, kind],
-            device_id=neighbours[other], device_id_type=MESH)
-
-    def x_copies(turn):
-        return [copy_of(turn, xs_ref.at[turn, d], xr_ref.at[turn, d], d, d) for d in range(2)]
-
-    def y_copies(turn, group):
-        return [
-            copy_of(turn, ys_ref.at[turn, d, group], yr_ref.at[turn, d, group], 2 + 2 * d + group, 2 + d)
-            for d in range(2)
-        ]
-
     def send_x(turn):
         for d, copy in enumerate(x_copies(turn)):
             x = 7 if d == 0 else 0
@@ -298,7 +363,7 @@
 
     def land_x(turn):
         for d, copy in enumerate(x_copies(turn)):
-            copy.wait()
+            copy.wait_recv()
             here = (gx > 0) if d == 0 else (gx < nx - 1)
             for j in range(8):
                 if j % 2 == 0:
@@ -308,7 +373,7 @@
 
     def land_y(turn, group):
         for d, copy in enumerate(y_copies(turn, group)):
-            copy.wait()
+            copy.wait_recv()
             here = (gy > 0) if d == 0 else (gy < ny - 1)
             rows = jnp.where(here, yr_ref[turn, d, group].astype(F32), 0.0)
             for j in range(2):
@@ -316,14 +381,12 @@
                     line = rows[8 * j + n : 8 * j + n + 1]
                     place(x, 49 + 2 * d + j, jnp.broadcast_to(line, (8, 256)))
 
-    def padded_tile(b, px):
+    def padded_tile(near_by, px):
         dx = -1 if px == 0 else (1 if px == 9 else 0)
         x = 7 if px == 0 else (0 if px == 9 else px - 1)
 
         def at(dy, dz):
-            if dx == 0 and dy == 0 and dz == 0:
-                return b + 1
-            return adj_ref[b, column_of(dx, dy, dz)] + 1
+            return near_by[dx, dy, dz]
 
         mid = tile_ref[x, at(0, 0)]
         low = pltpu.roll(jnp.where(row8 == 7, tile_ref[x, at(-1, 0)], mid), 1, 0)
@@ -338,9 +401,18 @@
         return jnp.concatenate([low, mid, high, emid, ehigh], axis=1)
 
     def pad_planes(planes):
+        steps = sorted({-1 if px == 0 else (1 if px == 9 else 0) for px in planes})
+
+        def slots(b):
+            return {
+                (dx, dy, dz): b + 1 if dx == dy == dz == 0 else adj_ref[b, column_of(dx, dy, dz)] + 1
+                for dx in steps for dy in (-1, 0, 1) for dz in (-1, 0, 1)
+            }
+
         def per_pair(n, carry):
+            even, odd = slots(2 * n), slots(2 * n + 1)
             for px in planes:
-                two = jnp.concatenate([padded_tile(2 * n, px), padded_tile(2 * n + 1, px)], axis=0)
+                two = jnp.concatenate([padded_tile(even, px), padded_tile(odd, px)], axis=0)
                 pad_ref[px, pl.ds(pl.multiple_of(16 * n, 16), 16), :] = two.astype(BF16)
             return carry
 
@@ -353,21 +425,19 @@
         land_y(turn, 1)
         pad_planes([x + 1 for x in GROUPS[1]])
 
-    def conv(pair, band_ref, bias):
+    def conv(first_plane, planes, band_ref, bias):
         total = bias_ref[pl.ds(bias, 1)]
         for i in range(3):
-            rows = pad_ref[pl.ds(2 * pair + i, 2)].reshape(512, 1024)
+            rows = pad_ref[pl.ds(first_plane + i, planes)].reshape(256 * planes, 1024)
             total = total + jnp.dot(rows, band_ref[i], preferred_element_type=F32)
         return total
 
-    send_x(0)
-    send_y(0, 0)
-    send_y(0, 1)
     land_and_pad(0)
 
     def first(pair):
-        v = conv(pair, band1_ref, 0)
-        h = (v / (1.0 + jnp.exp(-v))).astype(BF16).astype(F32)
+        v = conv(2 * pair, 2, band1_ref, 0)
+        half = 0.5 * v
+        h = (half + half * jnp.tanh(half)).astype(BF16).astype(F32)
         tile_ref[pl.ds(2 * pair, 2), pl.ds(1, NB)] = h.reshape(2, NB, 8, 256)
         e = edge_lanes(h[:, :128], h[:, 128:])
         edge_ref[pl.ds(2 * pair, 2), pl.ds(1, NB)] = e.reshape(2, NB, 8, 128)
@@ -385,10 +455,10 @@
     land_and_pad(1)
 
     def second(pair, carry):
-        sum_ref[pl.ds(2 * pair, 2)] = conv(pair, band2_ref, 1).reshape(2, NB, 8, 256)
-        return carry
-
-    lax.fori_loop(0, 4, second, 0)
+        sum_ref[pl.ds(4 * pair, 4)] = conv(4 * pair, 4, band2_ref, 1).reshape(4, NB, 8, 256)
+        return carry
+
+    lax.fori_loop(0, 2, second, 0)
 
     def finish(g, carry):
         rows = pl.ds(pl.multiple_of(256 * g, 256), 256)
@@ -398,20 +468,33 @@
             turned = jnp.concatenate([t[:, :128] for t in tall] + [t[:, 128:] for t in tall], axis=0).T
             parts.append(jnp.concatenate([turned[32 * k : 32 * k + 32] for k in range(4)], axis=1))
         total = jnp.concatenate(parts, axis=0) + level_ref[rows, :].astype(F32)
-        out_ref[rows, :] = total.astype(BF16)
+        rows = jnp.dot(total.astype(BF16), unperm_ref[...], preferred_element_type=F32).astype(BF16)
+        bricks = pl.ds(pl.multiple_of(8 * g, 8), 8)
+        fine_ref[bricks] = rows.reshape(8, 32, 512)
+        pltpu.make_async_copy(fine_ref.at[bricks], out_hbm.at[bricks], out_sem).start()
         return carry
 
     lax.fori_loop(0, 4, finish, 0)
-
-
-def reorder(values_ref, perm_ref, out_ref):
-    def part(g, carry):
-        rows = values_ref[pl.ds(pl.multiple_of(256 * g, 256), 256)]
-        rows = jnp.dot(rows, perm_ref[...], preferred_element_type=F32).astype(BF16)
-        out_ref[pl.ds(8 * g, 8)] = rows.reshape(8, 32, 512)
-        return carry
-
-    lax.fori_loop(0, 4, part, 0)
+    for turn in range(2):
+        for copy in x_copies(turn) + y_copies(turn, 0) + y_copies(turn, 1):
+            copy.wait_send()
+    wait_bytes(codes_ref.at[pl.ds(0, near - 1)], pair_sem.at[0])
+    wait_bytes(codes_ref.at[pl.ds(0, near * (far - 1))], block_sem.at[0])
+    wait_bytes(ret_ref.at[pl.ds(0, 2 * devices - 2)], reply_sem.at[0])
+    pltpu.make_async_copy(fine_ref, out_hbm, out_sem).wait()
+
+
+def hand_on(values_hbm, out_hbm, held, sem):
+    parts = [pl.ds(4 * n, 4) for n in range(8)]
+    into = [pltpu.make_async_copy(values_hbm.at[p], held.at[p], sem.at[0, n]) for n, p in enumerate(parts)]
+    onward = [pltpu.make_async_copy(held.at[p], out_hbm.at[p], sem.at[1, n]) for n, p in enumerate(parts)]
+    for copy in into:
+        copy.start()
+    for before, after in zip(into, onward):
+        before.wait()
+        after.start()
+    for copy in onward:
+        copy.wait()
 
 
 def per_device(
@@ -420,27 +503,40 @@
 ):
     devices = lax.axis_size("gx") * lax.axis_size("gy")
     perm, up = lane_tables()
-    vmem = pl.BlockSpec(memory_space=pltpu.VMEM)
-    smem = pl.BlockSpec(memory_space=pltpu.SMEM)
+    pick, pickup = face_tables()
     hbm = pl.BlockSpec(memory_space=pl.ANY)
     out = pl.pallas_call(
         kernel,
-        out_shape=jax.ShapeDtypeStruct((NB * 32, 512), BF16),
-        in_specs=[smem] * 6 + [vmem] * 3 + [hbm] * 4,
-        out_specs=vmem,
+        out_shape=jax.ShapeDtypeStruct((NB, 32, 512), BF16),
+        in_specs=[hbm] * 16,
+        out_specs=hbm,
         scratch_shapes=[
+            pltpu.SMEM((NB,), jnp.int32),
+            pltpu.SMEM((NB,), jnp.int32),
+            pltpu.SMEM((20,), jnp.int32),
+            pltpu.SMEM((NB, 26), jnp.int32),
+            pltpu.SMEM((32,), F32),
+            pltpu.SMEM((32,), F32),
+            pltpu.VMEM((32, 32), BF16),
+            pltpu.VMEM((27, 32, 32), BF16),
+            pltpu.VMEM((27, 32, 32), BF16),
             pltpu.VMEM((NB, 32, 512), BF16),
             pltpu.VMEM((512, 2048), BF16),
             pltpu.VMEM((512, 512), BF16),
+            pltpu.VMEM((512, 512), BF16),
             pltpu.VMEM((128, 1024), BF16),
+            pltpu.VMEM((2, 512, 128), BF16),
+            pltpu.VMEM((2, 128, 256), BF16),
             pltpu.VMEM((8, 128), jnp.int32),
             pltpu.VMEM((devices, 128), jnp.int32),
-            pltpu.VMEM((2 * devices, 512), BF16),
-            pltpu.VMEM((32 * devices, 128), F32),
+            pltpu.VMEM((2, devices, 512), BF16),
+            pltpu.VMEM((2, 16 * devices, 128), F32),
             pltpu.VMEM((2 * devices, 16, 128), BF16),
             pltpu.VMEM((2 * devices, 16, 128), BF16),
             pltpu.SMEM((NB,), jnp.int32),
             pltpu.VMEM((NB * 32, 512), F32),
+            pltpu.VMEM((3, 8, 32, 512), BF16),
+            pltpu.VMEM((3, 256, 128), F32),
             pltpu.VMEM((8, SLOTS, 8, 256), F32),
             pltpu.VMEM((8, SLOTS, 8, 128), F32),
             pltpu.VMEM((10, 256, 1024), BF16),
@@ -454,11 +550,13 @@
             pltpu.VMEM((2, 2, 64, 256), BF16),
             pltpu.VMEM((2, 2, 2, 16, 256), BF16),
             pltpu.VMEM((16, 256), F32),
+            pltpu.VMEM((16, 256), F32),
             pltpu.VMEM((2, 2, 64, 256), BF16),
             pltpu.VMEM((2, 2, 2, 16, 256), BF16),
             pltpu.SemaphoreType.DMA((2, 6)),
             pltpu.SemaphoreType.DMA((2, 6)),
-            pltpu.SemaphoreType.DMA((4,)),
+            pltpu.SemaphoreType.DMA((16,)),
+            pltpu.SemaphoreType.DMA,
             pltpu.SemaphoreType.DMA((2,)),
             pltpu.SemaphoreType.DMA((2,)),
             pltpu.SemaphoreType.DMA((2,)),
@@ -468,14 +566,17 @@
         ),
     )(
         parent_owner.reshape(NB), parent_cell, face_list, adjacency, bias_first, bias_second, parent_proj, conv_first,
-        conv_second, fine_features, coarse_cache, jnp.asarray(perm, BF16), jnp.asarray(up, BF16),
+        conv_second, fine_features, coarse_cache, jnp.asarray(perm, BF16),
+        jnp.asarray(perm.T, BF16), jnp.asarray(up, BF16),
+        jnp.asarray(pick, BF16), jnp.asarray(pickup, BF16),
     )
     return pl.pallas_call(
-        reorder,
+        hand_on,
         out_shape=jax.ShapeDtypeStruct((NB, 32, 512), BF16),
-        in_specs=[vmem] * 2,
-        out_specs=vmem,
-    )(out, jnp.asarray(perm.T, BF16))
+        in_specs=[hbm],
+        out_specs=hbm,
+        scratch_shapes=[pltpu.VMEM((NB, 32, 512), BF16), pltpu.SemaphoreType.DMA((2, 8))],
+    )(out)
 
 
 def solution(mesh):

time: 63.7 us -> 57.2 us (0.90)
  Pallas kernels: 63.5 us -> 56.9 us
    pallas_call x2, Pallas kernels: 63.5 us -> 56.9 us  [the longest x1 54.8 us: per_device(): pl.pallas_call(kernel, out_shape=jax.ShapeDtypeStruct((NB, 32, 512), BF16...]
where the time goes in v4:
time: 57.2 us; the launch traced here: 56.9 us
  Pallas kernels  56.9 us (99%)
    pallas_call x1, Pallas kernels, per_device(): pl.pallas_call(kernel, out_shape=jax.ShapeDtypeStruct((NB, 32, 512), BF16...  54.8 us
    pallas_call x1, Pallas kernels, per_device(): pl.pallas_call(hand_on, out_shape=jax.ShapeDtypeStruct((NB, 32, 512), BF1...  2.09 us

profile of v4, /device:TPU:0, one launch (start us, length us, event | category | flops | bytes accessed | tf_op | source)
XLA Modules:
  0.0 56.9 jit_solution(7063173072016173109)
XLA Ops:
  0.0 54.8 %shard_map.154.values_hbm = bf16[32,32,512]{2,1,0:T(8,128)(2,1)} custom-call(s32[32]{0:T(128)} %bitcast.1, s32[32]{0:T(128)} %cell_hbm.1, s32[20]{0:T(128)} %face_hbm.1, s32[32,26]{1,0:T(8,128)} %adj_hbm.1, f32[32]{0:T(128)} %bias1_hbm.1, f32[32]{0:T(128)} %bias2_hbm.1, bf16[32,32]{1,0:T(8,128)(2,1)} %proj_hbm.1, bf16[27,32,32]{2,1,0:T(8,128)(2,1)} %weight1_hbm.1, ...), custom_call_target="tpu_custom_call" | custom-call | tf_op jit(solution)/shard_map/pallas_call | solution.py:508
  54.8 2.1 %shard_map.155 = bf16[32,32,512]{2,1,0:T(8,128)(2,1)} custom-call(bf16[32,32,512]{2,1,0:T(8,128)(2,1)} %shard_map.154.values_hbm), custom_call_target="tpu_custom_call" | custom-call | tf_op jit(solution)/shard_map/pallas_call | solution.py:573

commit v5 on v4

--- a/solution.py
+++ b/solution.py
@@ -21,8 +21,8 @@
 
 def lane_tables():
     lane = np.arange(512)
-    z = 4 * (lane // 64 % 2) + lane // 128
-    x, y = lane % 64 // 8, lane % 8
+    x, row = lane % 64 // 8, lane % 8
+    y, z = 2 * (row // 2) + lane // 64 % 2, 4 * (row % 2) + lane // 128
     voxel = 64 * x + 8 * y + z
     cell = 16 * (x // 2) + 4 * (y // 2) + z // 2
     perm = (np.arange(512)[:, None] == voxel[None, :]).astype(np.float32)
@@ -35,9 +35,12 @@
 
 def face_tables():
     lane = np.arange(128)
-    fixed, z, free = np.where(lane < 64, 7, 0), lane % 64 // 8, lane % 8
+    fixed, at = np.where(lane < 64, 7, 0), lane % 64
+    part, row = at // 8, at % 8
+    across_x = (fixed, 2 * (row // 2) + part // 4, 4 * (row % 2) + part % 4)
+    across_y = (at % 16 // 2, fixed, 4 * (at % 2) + at // 16)
     picks, ups = [], []
-    for x, y in ((fixed, free), (free, fixed)):
+    for x, y, z in (across_x, across_y):
         voxel = 64 * x + 8 * y + z
         cell = 16 * (x // 2) + 4 * (y // 2) + z // 2
         picks.append((np.arange(512)[:, None] == voxel[None, :]).astype(np.float32))
@@ -48,37 +51,36 @@
 
 
 def build_band(weight_ref, band_ref):
-    lane = lax.broadcasted_iota(jnp.int32, (32, 256), 1)
-    zero = jnp.zeros((32, 256), F32)
+    block = lax.broadcasted_iota(jnp.int32, (32, 128), 1) // 32
+    zero = jnp.zeros((32, 128), F32)
 
     def per_x(i, carry):
-        first, last = [], []
+        moved = {}
         for j in range(3):
             taps = [weight_ref[9 * i + 3 * j + k].astype(F32) for k in (2, 1, 0)]
-            taps = jnp.concatenate(taps + [jnp.zeros((32, 32), F32)], axis=0)
-            strip = jnp.concatenate([taps.T, jnp.zeros((32, 128), F32)], axis=1)
-            for z in range(8):
-                rolled = strip if z == 1 else pltpu.roll(strip, (32 * (z - 1)) % 256, 1)
-                if z == 0:
-                    first.append(jnp.where(lane >= 224, rolled, zero))
-                    rolled = jnp.where(lane >= 224, zero, rolled)
-                if z == 7:
-                    last.append(jnp.where(lane < 32, rolled, zero))
-                    rolled = jnp.where(lane < 32, zero, rolled)
-                band_ref[i, pl.ds(256 * j + 32 * z, 32), :] = rolled.astype(BF16)
-        order = [first[0], first[1], last[1], last[0], first[2], zero, zero, last[2]]
-        for n, part in enumerate(order):
-            band_ref[i, pl.ds(768 + 32 * n, 32), :] = part.astype(BF16)
+            strip = jnp.concatenate(taps + [jnp.zeros((32, 32), F32)], axis=0).T
+            for z in range(-1, 5):
+                rolled = strip if z == 1 else pltpu.roll(strip, (32 * (z - 1)) % 128, 1)
+                fits = (block >= z - 1) & (block <= z + 1)
+                moved[j, z] = jnp.where(fits, rolled, 0.0)
+        order = [(y, z) for y in (0, 1, -1, 2) for z in range(4)]
+        order += [(0, 4), (1, 4), (0, -1), (1, -1), (2, 4), (-1, 4), (2, -1), (-1, -1)]
+        for n, (y, z) in enumerate(order):
+            halves = [moved[y + 1, z] if y < 2 else zero, moved[y, z] if y > -1 else zero]
+            band_ref[i, pl.ds(32 * n, 32), :] = jnp.concatenate(halves, axis=1).astype(BF16)
         return carry
 
     lax.fori_loop(0, 3, per_x, 0)
 
 
 def edge_lanes(low, high):
-    lane = lax.broadcasted_iota(jnp.int32, low.shape, 1)
-    a = jnp.where(lane < 32, low, pltpu.roll(low, 32, 1))
-    b = jnp.where(lane < 96, pltpu.roll(high, 96, 1), high)
-    return jnp.where(lane < 64, a, b)
+    axes = low.ndim
+    lane = lax.broadcasted_iota(jnp.int32, low.shape, axes - 1)
+    row = lax.broadcasted_iota(jnp.int32, low.shape, axes - 2)
+    a = jnp.where(lane < 32, low, pltpu.roll(high, 32, axes - 1))
+    b = jnp.where(lane < 96, pltpu.roll(low, 96, axes - 1), high)
+    ends = jnp.where(lane < 64, a, b)
+    return jnp.where(row % 2 == 0, pltpu.roll(ends, 7, axes - 2), pltpu.roll(ends, 1, axes - 2))
 
 
 def wait_bytes(ref, sem):
@@ -289,8 +291,10 @@
         for n in range(8 if group < 2 else 4):
             side = 64 * (group if group < 2 else n // 2)
             source = turned[n // 4]
+            tall = 8 if group < 2 else 16
             tiles.append(jnp.concatenate(
-                [source[side + 8 * z : side + 8 * z + 8, 32 * (n % 4) : 32 * (n % 4) + 32] for z in range(8)], axis=1
+                [source[side + at : side + at + tall, 32 * (n % 4) : 32 * (n % 4) + 32] for at in range(0, 64, tall)],
+                axis=1,
             ))
         return tiles
 
@@ -301,11 +305,10 @@
     lines = side_tiles(2)
     for d in range(2):
         for j in range(2):
-            yrow_ref[pl.ds(8 * j, 8), :] = lines[2 * d + j]
+            yrow_ref[:, pl.ds(128 * j, 128)] = lines[2 * d + j]
         for group in range(2):
-            for j in range(2):
-                for n, x in enumerate(GROUPS[group]):
-                    row_ref[pl.ds(8 * j + n, 1), :] = yrow_ref[pl.ds(8 * j + x, 1), :]
+            for n, x in enumerate(GROUPS[group]):
+                row_ref[pl.ds(2 * n, 2), :] = yrow_ref[pl.ds(2 * x, 2), :]
             ys_ref[0, d, group] = row_ref[...].astype(BF16)
     for group in range(2):
         for copy in y_copies(0, group):
@@ -337,9 +340,9 @@
 
     lax.fori_loop(0, 4, level, 0)
 
-    row8 = lax.broadcasted_iota(jnp.int32, (8, 256), 0)
-    row8e = lax.broadcasted_iota(jnp.int32, (8, 128), 0)
-    lane8e = lax.broadcasted_iota(jnp.int32, (8, 128), 1)
+    row8 = lax.broadcasted_iota(jnp.int32, (8, 128), 0)
+    lane8 = lax.broadcasted_iota(jnp.int32, (8, 128), 1)
+    inner = (lane8 < 64) == (row8 % 2 == 0)
 
     def send_x(turn):
         for d, copy in enumerate(x_copies(turn)):
@@ -353,11 +356,11 @@
 
     def send_y(turn, group):
         for d, copy in enumerate(y_copies(turn, group)):
-            y = 7 if d == 0 else 0
+            row, side = (6, 128) if d == 0 else (0, 0)
             for j in range(2):
                 at = face_ref[16 + 2 * d + j] + 1
                 for n, x in enumerate(GROUPS[group]):
-                    yrow_ref[pl.ds(8 * j + n, 1), :] = tile_ref[x, at, pl.ds(y, 1), :]
+                    yrow_ref[pl.ds(2 * n, 2), pl.ds(128 * j, 128)] = tile_ref[x, at, pl.ds(row, 2), pl.ds(side, 128)]
             ys_ref[turn, d, group] = yrow_ref[...].astype(BF16)
             copy.start()
 
@@ -378,8 +381,10 @@
             rows = jnp.where(here, yr_ref[turn, d, group].astype(F32), 0.0)
             for j in range(2):
                 for n, x in enumerate(GROUPS[group]):
-                    line = rows[8 * j + n : 8 * j + n + 1]
-                    place(x, 49 + 2 * d + j, jnp.broadcast_to(line, (8, 256)))
+                    lines = rows[2 * n : 2 * n + 2, 128 * j : 128 * j + 128]
+                    even = jnp.broadcast_to(lines[:1], (8, 128))
+                    half = jnp.where(row8 % 2 == 0, even, jnp.broadcast_to(lines[1:], (8, 128)))
+                    place(x, 49 + 2 * d + j, jnp.concatenate([half, half], axis=1))
 
     def padded_tile(near_by, px):
         dx = -1 if px == 0 else (1 if px == 9 else 0)
@@ -388,17 +393,20 @@
         def at(dy, dz):
             return near_by[dx, dy, dz]
 
+        def ends(dy):
+            outer = jnp.where(lane8 < 64, edge_ref[x, at(dy, 1)], edge_ref[x, at(dy, -1)])
+            return jnp.where(inner, edge_ref[x, at(dy, 0)], outer)
+
         mid = tile_ref[x, at(0, 0)]
-        low = pltpu.roll(jnp.where(row8 == 7, tile_ref[x, at(-1, 0)], mid), 1, 0)
-        high = pltpu.roll(jnp.where(row8 == 0, tile_ref[x, at(1, 0)], mid), 7, 0)
-        ends = [
-            jnp.where(lane8e < 64, edge_ref[x, at(dy, 1)], edge_ref[x, at(dy, -1)])
-            for dy in (-1, 0, 1)
-        ]
-        elow = pltpu.roll(jnp.where(row8e == 7, ends[0], ends[1]), 1, 0)
-        ehigh = pltpu.roll(jnp.where(row8e == 0, ends[2], ends[1]), 7, 0)
-        emid = jnp.where((lane8e >= 32) & (lane8e < 96), ends[1], elow)
-        return jnp.concatenate([low, mid, high, emid, ehigh], axis=1)
+        below = tile_ref[x, at(-1, 0), :, pl.ds(128, 128)]
+        above = tile_ref[x, at(1, 0), :, pl.ds(0, 128)]
+        low = pltpu.roll(jnp.where(row8 >= 6, below, mid[:, 128:]), 2, 0)
+        high = pltpu.roll(jnp.where(row8 < 2, above, mid[:, :128]), 6, 0)
+        here = ends(0)
+        clow = pltpu.roll(jnp.where(row8 >= 6, ends(-1), here), 2, 0)
+        chigh = pltpu.roll(jnp.where(row8 < 2, ends(1), here), 6, 0)
+        corners = jnp.where(lane8 // 32 % 2 == 1, clow, chigh)
+        return jnp.concatenate([mid, low, high, here, corners], axis=1)
 
     def pad_planes(planes):
         steps = sorted({-1 if px == 0 else (1 if px == 9 else 0) for px in planes})
@@ -428,7 +436,7 @@
     def conv(first_plane, planes, band_ref, bias):
         total = bias_ref[pl.ds(bias, 1)]
         for i in range(3):
-            rows = pad_ref[pl.ds(first_plane + i, planes)].reshape(256 * planes, 1024)
+            rows = pad_ref[pl.ds(first_plane + i, planes)].reshape(256 * planes, 768)
             total = total + jnp.dot(rows, band_ref[i], preferred_element_type=F32)
         return total
 
@@ -439,7 +447,7 @@
         half = 0.5 * v
         h = (half + half * jnp.tanh(half)).astype(BF16).astype(F32)
         tile_ref[pl.ds(2 * pair, 2), pl.ds(1, NB)] = h.reshape(2, NB, 8, 256)
-        e = edge_lanes(h[:, :128], h[:, 128:])
+        e = edge_lanes(h[:, :128].reshape(2 * NB, 8, 128), h[:, 128:].reshape(2 * NB, 8, 128))
         edge_ref[pl.ds(2 * pair, 2), pl.ds(1, NB)] = e.reshape(2, NB, 8, 128)
 
     def outer(n, carry):
@@ -539,9 +547,9 @@
             pltpu.VMEM((3, 256, 128), F32),
             pltpu.VMEM((8, SLOTS, 8, 256), F32),
             pltpu.VMEM((8, SLOTS, 8, 128), F32),
-            pltpu.VMEM((10, 256, 1024), BF16),
-            pltpu.VMEM((3, 1024, 256), BF16),
-            pltpu.VMEM((3, 1024, 256), BF16),
+            pltpu.VMEM((10, 256, 768), BF16),
+            pltpu.VMEM((3, 768, 256), BF16),
+            pltpu.VMEM((3, 768, 256), BF16),
             pltpu.VMEM((NB * 32, 512), BF16),
             pltpu.VMEM((NB * 16, 128), BF16),
             pltpu.VMEM((8, NB, 8, 256), F32),

time: 57.2 us -> 55.7 us (0.974)
  Pallas kernels: 56.9 us -> 55.4 us
    pallas_call x1, Pallas kernels: 54.8 us -> 53.3 us  [per_device(): pl.pallas_call(kernel, out_shape=jax.ShapeDtypeStruct((NB, 32, 512), BF16...]
where the time goes in v5:
time: 55.7 us; the launch traced here: 55.4 us
  Pallas kernels  55.4 us (99%)
    pallas_call x1, Pallas kernels, per_device(): pl.pallas_call(kernel, out_shape=jax.ShapeDtypeStruct((NB, 32, 512), BF16...  53.3 us
    pallas_call x1, Pallas kernels, per_device(): pl.pallas_call(hand_on, out_shape=jax.ShapeDtypeStruct((NB, 32, 512), BF1...  2.09 us

profile of v5, /device:TPU:0, one launch (start us, length us, event | category | flops | bytes accessed | tf_op | source)
XLA Modules:
  0.0 55.4 jit_solution(8691477916633790729)
XLA Ops:
  0.0 53.3 %shard_map.154.values_hbm = bf16[32,32,512]{2,1,0:T(8,128)(2,1)} custom-call(s32[32]{0:T(128)} %bitcast.1, s32[32]{0:T(128)} %cell_hbm.1, s32[20]{0:T(128)} %face_hbm.1, s32[32,26]{1,0:T(8,128)} %adj_hbm.1, f32[32]{0:T(128)} %bias1_hbm.1, f32[32]{0:T(128)} %bias2_hbm.1, bf16[32,32]{1,0:T(8,128)(2,1)} %proj_hbm.1, bf16[27,32,32]{2,1,0:T(8,128)(2,1)} %weight1_hbm.1, ...), custom_call_target="tpu_custom_call" | custom-call | tf_op jit(solution)/shard_map/pallas_call | solution.py:516
  53.3 2.1 %shard_map.155 = bf16[32,32,512]{2,1,0:T(8,128)(2,1)} custom-call(bf16[32,32,512]{2,1,0:T(8,128)(2,1)} %shard_map.154.values_hbm), custom_call_target="tpu_custom_call" | custom-call | tf_op jit(solution)/shard_map/pallas_call | solution.py:581

commit v6 on v5

--- a/solution.py
+++ b/solution.py
@@ -92,7 +92,7 @@
     fine_hbm, cache_hbm, perm_hbm, unperm_hbm, up_hbm, pick_hbm, pickup_hbm, out_hbm,
     owner_ref, cell_ref, face_ref, adj_ref, bias1_ref, bias2_ref, proj_ref, weight1_ref, weight2_ref,
     fine_ref, cache_ref, perm_ref, unperm_ref, up_ref, pick_ref, pickup_ref, code_ref, codes_ref, hot_ref, ans_ref, stage_ref, ret_ref, rank_ref,
-    finep_ref, side_ref, sidep_ref, tile_ref, edge_ref, pad_ref, band1_ref, band2_ref, level_ref, par_ref,
+    finep_ref, side_ref, sidep_ref, tile_ref, pad_ref, band1_ref, band2_ref, level_ref, par_ref,
     sum_ref, mix_ref, bias_ref, xs_ref, ys_ref, yrow_ref, row_ref, xr_ref, yr_ref,
     send_sem, recv_sem, load_sem, out_sem, pair_sem, block_sem, reply_sem,
 ):
@@ -217,6 +217,8 @@
             same = (owner_ref[other] == owner_ref[b]) & (other < b)
             count = count + jnp.where(same, 1, 0)
         rank_ref[b] = owner_ref[b] * 2 + count
+        for column in range(26):
+            adj_ref[b, column] = adj_ref[b, column] + 1
         return carry
 
     lax.fori_loop(0, NB, ranks, 0)
@@ -225,8 +227,7 @@
     yrow_ref[...] = jnp.zeros_like(yrow_ref)
     row_ref[...] = jnp.zeros_like(row_ref)
     for x in range(8):
-        tile_ref[x, 0] = jnp.zeros((8, 256), F32)
-        edge_ref[x, 0] = jnp.zeros((8, 128), F32)
+        tile_ref[x, 0] = jnp.zeros((8, 384), F32)
     lane = lax.broadcasted_iota(jnp.int32, (1, 256), 1)
     for n, ref in enumerate((bias1_ref, bias2_ref)):
         line = jnp.zeros((1, 256), F32)
@@ -263,8 +264,7 @@
     wait_bytes(ret_ref.at[pl.ds(0, 2 * devices - 2)], reply_sem.at[1])
 
     def place(x, slot, tile):
-        tile_ref[x, slot] = tile
-        edge_ref[x, slot] = edge_lanes(tile[:, :128], tile[:, 128:])
+        tile_ref[x, slot] = jnp.concatenate([tile, edge_lanes(tile[:, :128], tile[:, 128:])], axis=1)
 
     def copy_of(turn, src, dst, kind, other):
         return pltpu.make_async_remote_copy(
@@ -349,7 +349,7 @@
             x = 7 if d == 0 else 0
             for j in range(0, 8, 2):
                 two = jnp.concatenate(
-                    [tile_ref[x, face_ref[8 * d + j] + 1], tile_ref[x, face_ref[8 * d + j + 1] + 1]], axis=0
+                    [tile_ref[x, face_ref[8 * d + j + n] + 1, :, pl.ds(0, 256)] for n in range(2)], axis=0
                 )
                 xs_ref[turn, d, pl.ds(8 * j, 16), :] = two.astype(BF16)
             copy.start()
@@ -394,10 +394,10 @@
             return near_by[dx, dy, dz]
 
         def ends(dy):
-            outer = jnp.where(lane8 < 64, edge_ref[x, at(dy, 1)], edge_ref[x, at(dy, -1)])
-            return jnp.where(inner, edge_ref[x, at(dy, 0)], outer)
-
-        mid = tile_ref[x, at(0, 0)]
+            one, two, own = (tile_ref[x, at(dy, dz), :, pl.ds(256, 128)] for dz in (1, -1, 0))
+            return jnp.where(inner, own, jnp.where(lane8 < 64, one, two))
+
+        mid = tile_ref[x, at(0, 0), :, pl.ds(0, 256)]
         below = tile_ref[x, at(-1, 0), :, pl.ds(128, 128)]
         above = tile_ref[x, at(1, 0), :, pl.ds(0, 128)]
         low = pltpu.roll(jnp.where(row8 >= 6, below, mid[:, 128:]), 2, 0)
@@ -413,7 +413,7 @@
 
         def slots(b):
             return {
-                (dx, dy, dz): b + 1 if dx == dy == dz == 0 else adj_ref[b, column_of(dx, dy, dz)] + 1
+                (dx, dy, dz): b + 1 if dx == dy == dz == 0 else adj_ref[b, column_of(dx, dy, dz)]
                 for dx in steps for dy in (-1, 0, 1) for dz in (-1, 0, 1)
             }
 
@@ -440,15 +440,18 @@
             total = total + jnp.dot(rows, band_ref[i], preferred_element_type=F32)
         return total
 
-    land_and_pad(0)
+    land_x(0)
+    land_y(0, 0)
+    land_y(0, 1)
+    pad_planes(range(10))
 
     def first(pair):
         v = conv(2 * pair, 2, band1_ref, 0)
         half = 0.5 * v
         h = (half + half * jnp.tanh(half)).astype(BF16).astype(F32)
-        tile_ref[pl.ds(2 * pair, 2), pl.ds(1, NB)] = h.reshape(2, NB, 8, 256)
+        tile_ref[pl.ds(2 * pair, 2), pl.ds(1, NB), :, pl.ds(0, 256)] = h.reshape(2, NB, 8, 256)
         e = edge_lanes(h[:, :128].reshape(2 * NB, 8, 128), h[:, 128:].reshape(2 * NB, 8, 128))
-        edge_ref[pl.ds(2 * pair, 2), pl.ds(1, NB)] = e.reshape(2, NB, 8, 128)
+        tile_ref[pl.ds(2 * pair, 2), pl.ds(1, NB), :, pl.ds(256, 128)] = e.reshape(2, NB, 8, 128)
 
     def outer(n, carry):
         first(3 * n)
@@ -469,20 +472,20 @@
     lax.fori_loop(0, 2, second, 0)
 
     def finish(g, carry):
-        rows = pl.ds(pl.multiple_of(256 * g, 256), 256)
+        rows = pl.ds(pl.multiple_of(512 * g, 512), 512)
         parts = []
-        for n in range(8):
-            tall = [sum_ref[x, 8 * g + n] for x in range(8)]
+        for n in range(16):
+            tall = [sum_ref[x, 16 * g + n] for x in range(8)]
             turned = jnp.concatenate([t[:, :128] for t in tall] + [t[:, 128:] for t in tall], axis=0).T
             parts.append(jnp.concatenate([turned[32 * k : 32 * k + 32] for k in range(4)], axis=1))
         total = jnp.concatenate(parts, axis=0) + level_ref[rows, :].astype(F32)
         rows = jnp.dot(total.astype(BF16), unperm_ref[...], preferred_element_type=F32).astype(BF16)
-        bricks = pl.ds(pl.multiple_of(8 * g, 8), 8)
-        fine_ref[bricks] = rows.reshape(8, 32, 512)
+        bricks = pl.ds(pl.multiple_of(16 * g, 16), 16)
+        fine_ref[bricks] = rows.reshape(16, 32, 512)
         pltpu.make_async_copy(fine_ref.at[bricks], out_hbm.at[bricks], out_sem).start()
         return carry
 
-    lax.fori_loop(0, 4, finish, 0)
+    lax.fori_loop(0, 2, finish, 0)
     for turn in range(2):
         for copy in x_copies(turn) + y_copies(turn, 0) + y_copies(turn, 1):
             copy.wait_send()
@@ -545,8 +548,7 @@
             pltpu.VMEM((NB * 32, 512), F32),
             pltpu.VMEM((3, 8, 32, 512), BF16),
             pltpu.VMEM((3, 256, 128), F32),
-            pltpu.VMEM((8, SLOTS, 8, 256), F32),
-            pltpu.VMEM((8, SLOTS, 8, 128), F32),
+            pltpu.VMEM((8, SLOTS, 8, 384), F32),
             pltpu.VMEM((10, 256, 768), BF16),
             pltpu.VMEM((3, 768, 256), BF16),
             pltpu.VMEM((3, 768, 256), BF16),

time: 55.7 us -> 54.8 us (0.984)
  Pallas kernels: 55.4 us -> 54.5 us
    pallas_call x1, Pallas kernels: 53.3 us -> 52.4 us  [per_device(): pl.pallas_call(kernel, out_shape=jax.ShapeDtypeStruct((NB, 32, 512), BF16...]
where the time goes in v6:
time: 54.8 us; the launch traced here: 54.5 us
  Pallas kernels  54.5 us (99%)
    pallas_call x1, Pallas kernels, per_device(): pl.pallas_call(kernel, out_shape=jax.ShapeDtypeStruct((NB, 32, 512), BF16...  52.4 us
    pallas_call x1, Pallas kernels, per_device(): pl.pallas_call(hand_on, out_shape=jax.ShapeDtypeStruct((NB, 32, 512), BF1...  2.09 us

profile of v6, /device:TPU:0, one launch (start us, length us, event | category | flops | bytes accessed | tf_op | source)
XLA Modules:
  0.0 54.5 jit_solution(3225239006874088974)
XLA Ops:
  0.0 52.4 %shard_map.154.values_hbm = bf16[32,32,512]{2,1,0:T(8,128)(2,1)} custom-call(s32[32]{0:T(128)} %bitcast.1, s32[32]{0:T(128)} %cell_hbm.1, s32[20]{0:T(128)} %face_hbm.1, s32[32,26]{1,0:T(8,128)} %adj_hbm.1, f32[32]{0:T(128)} %bias1_hbm.1, f32[32]{0:T(128)} %bias2_hbm.1, bf16[32,32]{1,0:T(8,128)(2,1)} %proj_hbm.1, bf16[27,32,32]{2,1,0:T(8,128)(2,1)} %weight1_hbm.1, ...), custom_call_target="tpu_custom_call" | custom-call | tf_op jit(solution)/shard_map/pallas_call | solution.py:519
  52.4 2.1 %shard_map.155 = bf16[32,32,512]{2,1,0:T(8,128)(2,1)} custom-call(bf16[32,32,512]{2,1,0:T(8,128)(2,1)} %shard_map.154.values_hbm), custom_call_target="tpu_custom_call" | custom-call | tf_op jit(solution)/shard_map/pallas_call | solution.py:583

commit v7 on v6

--- a/solution.py
+++ b/solution.py
@@ -178,7 +178,7 @@
             ans_ref[turn, pl.ds(pl.multiple_of((2 * n + 1) * devices, devices), devices), :] = rows[:, 128:]
             return carry
 
-        lax.fori_loop(0, 8, answer, 0)
+        lax.fori_loop(0, 8, answer, 0, unroll=True)
 
         def answer_to(at):
             first = ans_ref[turn, pl.ds(at, 16, stride=devices), :]
@@ -424,7 +424,7 @@
                 pad_ref[px, pl.ds(pl.multiple_of(16 * n, 16), 16), :] = two.astype(BF16)
             return carry
 
-        lax.fori_loop(0, NB // 2, per_pair, 0)
+        lax.fori_loop(0, NB // 2, per_pair, 0, unroll=2)
 
     def land_and_pad(turn):
         land_x(turn)

time: 54.8 us -> 53.5 us (0.976)
  Pallas kernels: 54.5 us -> 53.2 us
    pallas_call x1, Pallas kernels: 52.4 us -> 51.1 us  [per_device(): pl.pallas_call(kernel, out_shape=jax.ShapeDtypeStruct((NB, 32, 512), BF16...]
where the time goes in v7:
time: 53.5 us; the launch traced here: 53.2 us
  Pallas kernels  53.2 us (99%)
    pallas_call x1, Pallas kernels, per_device(): pl.pallas_call(kernel, out_shape=jax.ShapeDtypeStruct((NB, 32, 512), BF16...  51.1 us
    pallas_call x1, Pallas kernels, per_device(): pl.pallas_call(hand_on, out_shape=jax.ShapeDtypeStruct((NB, 32, 512), BF1...  2.09 us

profile of v7, /device:TPU:0, one launch (start us, length us, event | category | flops | bytes accessed | tf_op | source)
XLA Modules:
  0.0 53.2 jit_solution(14213117436369573080)
XLA Ops:
  0.0 51.1 %shard_map.154.values_hbm = bf16[32,32,512]{2,1,0:T(8,128)(2,1)} custom-call(s32[32]{0:T(128)} %bitcast.1, s32[32]{0:T(128)} %cell_hbm.1, s32[20]{0:T(128)} %face_hbm.1, s32[32,26]{1,0:T(8,128)} %adj_hbm.1, f32[32]{0:T(128)} %bias1_hbm.1, f32[32]{0:T(128)} %bias2_hbm.1, bf16[32,32]{1,0:T(8,128)(2,1)} %proj_hbm.1, bf16[27,32,32]{2,1,0:T(8,128)(2,1)} %weight1_hbm.1, ...), custom_call_target="tpu_custom_call" | custom-call | tf_op jit(solution)/shard_map/pallas_call | solution.py:519
  51.1 2.1 %shard_map.155 = bf16[32,32,512]{2,1,0:T(8,128)(2,1)} custom-call(bf16[32,32,512]{2,1,0:T(8,128)(2,1)} %shard_map.154.values_hbm), custom_call_target="tpu_custom_call" | custom-call | tf_op jit(solution)/shard_map/pallas_call | solution.py:583

commit v8 on v7

--- a/solution.py
+++ b/solution.py
@@ -203,7 +203,7 @@
                 device_id=(dx, dy), device_id_type=MESH).start()
             return carry
 
-        lax.fori_loop(start, half, reply, 0)
+        lax.fori_loop(start, half, reply, 0, unroll=3 if start else 2)
 
     answers(0, core, 1)
     answers(1, 1 - core, 0)

time: 53.5 us -> 53.5 us (level)
  no operation moved by 1% of the time
where the time goes in v8:
time: 53.5 us; the launch traced here: 53.2 us
  Pallas kernels  53.2 us (99%)
    pallas_call x1, Pallas kernels, per_device(): pl.pallas_call(kernel, out_shape=jax.ShapeDtypeStruct((NB, 32, 512), BF16...  51.1 us
    pallas_call x1, Pallas kernels, per_device(): pl.pallas_call(hand_on, out_shape=jax.ShapeDtypeStruct((NB, 32, 512), BF1...  2.09 us

profile of v8, /device:TPU:0, one launch (start us, length us, event | category | flops | bytes accessed | tf_op | source)
XLA Modules:
  0.0 53.2 jit_solution(7115754202551073297)
XLA Ops:
  0.0 51.1 %shard_map.154.values_hbm = bf16[32,32,512]{2,1,0:T(8,128)(2,1)} custom-call(s32[32]{0:T(128)} %bitcast.1, s32[32]{0:T(128)} %cell_hbm.1, s32[20]{0:T(128)} %face_hbm.1, s32[32,26]{1,0:T(8,128)} %adj_hbm.1, f32[32]{0:T(128)} %bias1_hbm.1, f32[32]{0:T(128)} %bias2_hbm.1, bf16[32,32]{1,0:T(8,128)(2,1)} %proj_hbm.1, bf16[27,32,32]{2,1,0:T(8,128)(2,1)} %weight1_hbm.1, ...), custom_call_target="tpu_custom_call" | custom-call | tf_op jit(solution)/shard_map/pallas_call | solution.py:519
  51.1 2.1 %shard_map.155 = bf16[32,32,512]{2,1,0:T(8,128)(2,1)} custom-call(bf16[32,32,512]{2,1,0:T(8,128)(2,1)} %shard_map.154.values_hbm), custom_call_target="tpu_custom_call" | custom-call | tf_op jit(solution)/shard_map/pallas_call | solution.py:583
